TPU v7x, 32 devices: a whole 2x2x4 slice. The times are simulated.
32 devices in a mesh: seq: 8 (over z, y), chan: 4 (over x, core).
Axes of the slice: x: 2, y: 2, z: 4, core: 2. Of those that a mesh axis runs over, the one named last changes fastest.
Arguments:
- tokens: bfloat16 [8192, 512], P('seq', 'chan'), may hold values from -6 to 6
- w_in: bfloat16 [512, 3, 512], P(None, None, 'chan'), may hold values from -0.25 to 0.25
- short_filter: float32 [3, 3, 512], P(None, None, 'chan'), may hold values from -3 to 3
- long_filter: float32 [8192, 512], P('seq', 'chan'), may hold values from -0.0625 to 0.0625
- skip_gain: float32 [512], P('chan'), may hold values from 0.5 to 1.5
- w_out: bfloat16 [512, 512], P('chan'), may hold values from -0.25 to 0.25
Outputs:
- mixed: bfloat16 [8192, 512], P('seq', 'chan')
All inputs are finite; a program needn't handle non-finite values.
Results may differ from a plain program's by a relative error of at most 0.007.
Values may be sent and summed in bfloat16 or wider, within the bound.
A program may use at most 64 MiB of HBM per device.

v0:
```python
import math

import jax
import jax.numpy as jnp
from jax import lax
from jax.sharding import PartitionSpec as P


def swapped(block, axis, distance):
    count = lax.axis_size(axis)
    route = []
    for low in range(count):
        high = low | 1 << distance
        if high != low and high < count:
            route += [(low, high), (high, low)]
    return lax.ppermute(block, axis, route)


def shifted(block, axis, distance):
    devices = range(lax.axis_size(axis))
    route = [(i - distance, i) for i in devices if i - distance in devices]
    return lax.ppermute(block, axis, route)


def rotate(real_part, imag_part, angle):
    cosine = jnp.cos(angle)
    sine = jnp.sin(angle)
    return (real_part * cosine - imag_part * sine, real_part * sine + imag_part * cosine)


def dft_table(count):
    indices = jnp.arange(count, dtype=jnp.int32)
    product = indices[:, None] * indices[None, :] % count
    angle = 2.0 * math.pi / count * product.astype(jnp.float32)
    return (jnp.cos(angle), jnp.sin(angle))


def table_product(form, cosine, sine, real_part, imag_part, sign):
    highest = lax.Precision.HIGHEST
    cos_real = jnp.einsum(form, cosine, real_part, precision=highest)
    cos_imag = jnp.einsum(form, cosine, imag_part, precision=highest)
    sin_real = jnp.einsum(form, sine, real_part, precision=highest)
    sin_imag = jnp.einsum(form, sine, imag_part, precision=highest)
    return (cos_real - sign * sin_imag, cos_imag + sign * sin_real)


def transform(real_part, imag_part, sign):
    count = real_part.shape[-2]
    width = real_part.shape[-1]
    leading = real_part.shape[:-2]
    first = 1
    for factor in range(1, int(math.isqrt(count)) + 1):
        if count % factor == 0:
            first = factor
    second = count // first
    real_part = real_part.reshape(leading + (second, first, width))
    imag_part = imag_part.reshape(leading + (second, first, width))
    cos_second, sin_second = dft_table(second)
    real_part, imag_part = table_product(
        "kq,...qac->...kac", cos_second, sin_second, real_part, imag_part, sign
    )
    outer = jnp.arange(second, dtype=jnp.int32)
    within = jnp.arange(first, dtype=jnp.int32)
    phase = outer[:, None] * within[None, :] % count
    angle = sign * 2.0 * math.pi / count * phase.astype(jnp.float32)
    real_part, imag_part = rotate(real_part, imag_part, angle[:, :, None])
    cos_first, sin_first = dft_table(first)
    real_part, imag_part = table_product(
        "ja,...kac->...jkc", cos_first, sin_first, real_part, imag_part, sign
    )
    return (
        real_part.reshape(leading + (count, width)),
        imag_part.reshape(leading + (count, width)),
    )


def spectral(real_part, imag_part, column, count, total):
    positions = jnp.arange(count, dtype=jnp.int32)
    phase = column[:, None] * positions[None, :] % total
    angle = -2.0 * math.pi / total * phase.astype(jnp.float32)
    real_part, imag_part = rotate(real_part, imag_part, angle[:, None, :, None])
    spec_real, spec_imag = transform(real_part, imag_part, -1.0)
    prod_real = spec_real[:, 0] * spec_real[:, 1] - spec_imag[:, 0] * spec_imag[:, 1]
    prod_imag = spec_real[:, 0] * spec_imag[:, 1] + spec_imag[:, 0] * spec_real[:, 1]
    back_real, back_imag = transform(prod_real, prod_imag, 1.0)
    return rotate(back_real / count, back_imag / count, -angle[:, :, None])


def forward_section(real_part, imag_part, my_index, level):
    half = 1 << level
    upper = (my_index // half % 2).astype(jnp.float32)
    offset = (my_index % half).astype(jnp.float32)
    other_real, other_imag = swapped((real_part, imag_part), "seq", level)
    factor = 1.0 - 2.0 * upper
    return rotate(
        other_real + factor * real_part,
        other_imag + factor * imag_part,
        -math.pi * offset / half * upper,
    )


def inverse_section(real_part, imag_part, my_index, level):
    half = 1 << level
    upper = (my_index // half % 2).astype(jnp.float32)
    offset = (my_index % half).astype(jnp.float32)
    real_part, imag_part = rotate(real_part, imag_part, math.pi * offset / half * upper)
    other_real, other_imag = swapped((real_part, imag_part), "seq", level)
    factor = 1.0 - 2.0 * upper
    return (0.5 * (other_real + factor * real_part), 0.5 * (other_imag + factor * imag_part))


def butterfly_conv(signals, count):
    my_index = lax.axis_index("seq")
    shards = lax.axis_size("seq")
    levels = shards.bit_length() - 1
    top_angle = -math.pi * my_index.astype(jnp.float32) / shards
    zeros_part = jnp.zeros_like(signals)
    turned_real, turned_imag = rotate(signals, zeros_part, top_angle)
    real_part = jnp.stack([signals, turned_real])
    imag_part = jnp.stack([zeros_part, turned_imag])
    for level in reversed(range(levels)):
        real_part, imag_part = forward_section(real_part, imag_part, my_index, level)
    reversed_index = jnp.zeros((), jnp.int32)
    for level in range(levels):
        reversed_index = reversed_index + my_index // (1 << level) % 2 * (1 << levels - 1 - level)
    column = jnp.arange(2, dtype=jnp.int32) + 2 * reversed_index
    real_part, imag_part = spectral(real_part, imag_part, column, count, 2 * shards * count)
    for level in range(levels):
        real_part, imag_part = inverse_section(real_part, imag_part, my_index, level)
    back_real, back_imag = rotate(real_part[1], imag_part[1], -top_angle)
    return 0.5 * (real_part[0] + back_real)


def on_device(tokens, w_in, short_filter, long_filter, skip_gain, w_out):
    features = lax.all_gather(tokens, "chan", axis=1, tiled=True)
    projected = jnp.einsum(
        "tc,cgd->tgd", features, w_in, preferred_element_type=jnp.float32
    ).astype(jnp.bfloat16)
    rim_rows = shifted(projected[-2:], "seq", 1)
    extended = jnp.concatenate([rim_rows, projected], axis=0).astype(jnp.float32)
    short = (
        short_filter[0] * extended[2:]
        + short_filter[1] * extended[1:-1]
        + short_filter[2] * extended[:-2]
    )
    inner = short[:, 0, :] * short[:, 1, :]
    signals = jnp.stack([inner, long_filter])
    count = inner.shape[0]
    conv = butterfly_conv(signals, count)
    gated = (short[:, 2, :] * (conv + skip_gain * inner)).astype(jnp.bfloat16)
    terms = jnp.dot(gated, w_out, preferred_element_type=jnp.float32)
    return lax.psum_scatter(terms, "chan", scatter_dimension=1, tiled=True).astype(jnp.bfloat16)


def solution(mesh):
    return jax.shard_map(
        on_device,
        mesh=mesh,
        in_specs=(
            P("seq", "chan"),
            P(None, None, "chan"),
            P(None, None, "chan"),
            P("seq", "chan"),
            P("chan"),
            P("chan", None),
        ),
        out_specs=P("seq", "chan"),
        check_vma=False,
    )
```

profile of v0, /device:TPU:1, one launch (start us, length us, event | category | flops | bytes accessed | tf_op | source)
XLA Modules:
  0.0 698.5 jit_solution(2036189136092745113)
XLA Ops:
  7.3 21.0 %all-gather.2.cloned.1.call-done = bf16[1024,512]{1,0:T(8,128)(2,1)} async-done(((bf16[1024,128]{1,0:T(8,128)(2,1)}), bf16[1024,512]{1,0:T(8,128)(2,1)}) %all-gather.2.cloned.1.call-update) | async-done | bytes 1048592 | tf_op jit(solution)/shard_map/all_gather | solution.py:135
  37.9 3.5 collective-permute-start.1
  43.1 133.4 %collective-permute-done.1 = f32[2,2,1024,128]{3,2,1,0:T(8,128)} collective-permute-done((f32[2,2,1024,128]{3,2,1,0:T(8,128)}, f32[2,2,1024,128]{3,2,1,0:T(8,128)}, u32[]{:S(2)}, u32[]{:S(2)}) %collective-permute-start.1) | collective-permute-done | bytes 2097184 | tf_op jit(solution)/shard_map/ppermute | solution.py:16
  176.4 44.9 %collective-permute-done.2 = f32[2,2,1024,128]{3,2,1,0:T(8,128)} collective-permute-done((f32[2,2,1024,128]{3,2,1,0:T(8,128)}, f32[2,2,1024,128]{3,2,1,0:T(8,128)}, u32[]{:S(2)}, u32[]{:S(2)}) %collective-permute-start.2) | collective-permute-done | bytes 2097184 | tf_op jit(solution)/shard_map/ppermute | solution.py:16
  221.4 4.9 multiply_add_fusion.7
  228.2 44.6 %collective-permute-done.3 = f32[2,2,1024,128]{3,2,1,0:T(8,128)S(1)} collective-permute-done((f32[2,2,1024,128]{3,2,1,0:T(8,128)}, f32[2,2,1024,128]{3,2,1,0:T(8,128)S(1)}, u32[]{:S(2)}, u32[]{:S(2)}) %collective-permute-start.3) | collective-permute-done | bytes 2097184 | tf_op jit(solution)/shard_map/ppermute | solution.py:16
  274.2 43.5 %collective-permute-done.4 = f32[2,2,1024,128]{3,2,1,0:T(8,128)} collective-permute-done((f32[2,2,1024,128]{3,2,1,0:T(8,128)}, f32[2,2,1024,128]{3,2,1,0:T(8,128)}, u32[]{:S(2)}, u32[]{:S(2)}) %collective-permute-start.4) | collective-permute-done | bytes 2097184 | tf_op jit(solution)/shard_map/ppermute | solution.py:16
  317.7 5.6 multiply_subtract_fusion.3
  326.1 42.4 %collective-permute-done.5 = f32[2,2,1024,128]{3,2,1,0:T(8,128)} collective-permute-done((f32[2,2,1024,128]{3,2,1,0:T(8,128)S(1)}, f32[2,2,1024,128]{3,2,1,0:T(8,128)}, u32[]{:S(2)}, u32[]{:S(2)}) %collective-permute-start.5) | collective-permute-done | bytes 2097184 | tf_op jit(solution)/shard_map/ppermute | solution.py:16
  368.5 44.9 %collective-permute-done.6 = f32[2,2,1024,128]{3,2,1,0:T(8,128)} collective-permute-done((f32[2,2,1024,128]{3,2,1,0:T(8,128)}, f32[2,2,1024,128]{3,2,1,0:T(8,128)}, u32[]{:S(2)}, u32[]{:S(2)}) %collective-permute-start.6) | collective-permute-done | bytes 2097184 | tf_op jit(solution)/shard_map/ppermute | solution.py:16
  424.5 3.4 multiply_subtract_fusion
  427.9 4.2 fusion
  438.6 3.4 subtract_bitcast_fusion
  443.5 3.4 add_bitcast_fusion
  466.8 20.0 %collective-permute-done.7 = f32[2,1024,128]{2,1,0:T(8,128)S(1)} collective-permute-done((f32[2,1024,128]{2,1,0:T(8,128)S(1)}, f32[2,1024,128]{2,1,0:T(8,128)S(1)}, u32[]{:S(2)}, u32[]{:S(2)}) %collective-permute-start.7) | collective-permute-done | bytes 1048608 | tf_op jit(solution)/shard_map/ppermute | solution.py:16
  487.8 21.6 %collective-permute-done.8 = f32[2,1024,128]{2,1,0:T(8,128)} collective-permute-done((f32[2,1024,128]{2,1,0:T(8,128)S(1)}, f32[2,1024,128]{2,1,0:T(8,128)}, u32[]{:S(2)}, u32[]{:S(2)}) %collective-permute-start.8) | collective-permute-done | bytes 1048608 | tf_op jit(solution)/shard_map/ppermute | solution.py:16
  512.2 3.7 collective-permute-start.10
  516.1 20.1 %collective-permute-done.10 = f32[2,1024,128]{2,1,0:T(8,128)S(1)} collective-permute-done((f32[2,1024,128]{2,1,0:T(8,128)S(1)}, f32[2,1024,128]{2,1,0:T(8,128)S(1)}, u32[]{:S(2)}, u32[]{:S(2)}) %collective-permute-start.10) | collective-permute-done | bytes 1048608 | tf_op jit(solution)/shard_map/ppermute | solution.py:16
  537.2 21.6 %collective-permute-done.9 = f32[2,1024,128]{2,1,0:T(8,128)} collective-permute-done((f32[2,1024,128]{2,1,0:T(8,128)}, f32[2,1024,128]{2,1,0:T(8,128)}, u32[]{:S(2)}, u32[]{:S(2)}) %collective-permute-start.9) | collective-permute-done | bytes 1048608 | tf_op jit(solution)/shard_map/ppermute | solution.py:16
  561.0 4.2 collective-permute-start.11
  565.4 68.2 %collective-permute-done.11 = f32[2,1024,128]{2,1,0:T(8,128)S(1)} collective-permute-done((f32[2,1024,128]{2,1,0:T(8,128)S(1)}, f32[2,1024,128]{2,1,0:T(8,128)S(1)}, u32[]{:S(2)}, u32[]{:S(2)}) %collective-permute-start.11) | collective-permute-done | bytes 1048608 | tf_op jit(solution)/shard_map/ppermute | solution.py:16
  633.8 22.5 %collective-permute-done.12 = f32[2,1024,128]{2,1,0:T(8,128)} collective-permute-done((f32[2,1024,128]{2,1,0:T(8,128)S(1)}, f32[2,1024,128]{2,1,0:T(8,128)}, u32[]{:S(2)}, u32[]{:S(2)}) %collective-permute-start.12) | collective-permute-done | bytes 1048608 | tf_op jit(solution)/shard_map/ppermute | solution.py:16
  656.2 3.4 fusion.56
  659.7 29.8 %reduce-scatter.2.cloned.1.call-done = f32[1024,128]{1,0:T(8,128)} async-done(((f32[1024,512]{1,0:T(8,128)}), f32[1024,128]{1,0:T(8,128)}) %reduce-scatter.2.cloned.1.call-update) | async-done | bytes 524304 | tf_op jit(solution)/shard_map/reduce_scatter | solution.py:152
  (77 shorter events, 64.8 us)
Async XLA Ops:
  6.5 21.7 %copy-start = (bf16[512,3,128]{2,0,1:T(8,128)(2,1)S(1)}, bf16[512,3,128]{2,0,1:T(8,128)(2,1)}, u32[]{:S(2)}) copy-start(bf16[512,3,128]{2,0,1:T(8,128)(2,1)} %param.7) | copy-start | bytes 1179652
  6.5 26.8 %copy-start.7 = (f32[3,3,128]{2,1,0:T(4,128)S(1)}, f32[3,3,128]{2,1,0:T(4,128)}, u32[]{:S(2)}) copy-start(f32[3,3,128]{2,1,0:T(4,128)} %param.8) | copy-start | bytes 13828
  6.5 21.7 %all-gather.2.cloned.1.call-start = ((), (), s32[]{:S(2)}) async-start(), calls=%async_computation.1 | async-start | bytes 1310720 | tf_op jit(solution)/shard_map/all_gather | solution.py:135
  7.3 682.2 %reduce-scatter.2.cloned.1.call-start = ((), (), s32[]{:S(2)}) async-start(), calls=%async_computation.2 | async-start | bytes 2621440 | tf_op jit(solution)/shard_map/reduce_scatter | solution.py:152
  30.2 3.8 collective-permute-start
  34.7 1.5 copy-start.2
  34.7 1.4 copy-start.4
  37.9 138.6 %collective-permute-start.1 = (f32[2,2,1024,128]{3,2,1,0:T(8,128)}, f32[2,2,1024,128]{3,2,1,0:T(8,128)}, u32[]{:S(2)}, u32[]{:S(2)}) collective-permute-start(f32[2,2,1024,128]{3,2,1,0:T(8,128)} %pad_maximum_fusion), channel_id=1, source_target_pairs={{0,16},{16,0},{4,20},{20,4},{8,24},{24,8},{12,28},{28,12},{1,17},{... | collective-permute-start | bytes 6291464 | tf_op jit(solution)/shard_map/ppermute | solution.py:16
  42.9 178.5 %collective-permute-start.2 = (f32[2,2,1024,128]{3,2,1,0:T(8,128)}, f32[2,2,1024,128]{3,2,1,0:T(8,128)}, u32[]{:S(2)}, u32[]{:S(2)}) collective-permute-start(f32[2,2,1024,128]{3,2,1,0:T(8,128)} %stack.31), channel_id=1, source_target_pairs={{0,16},{16,0},{4,20},{20,4},{8,24},{24,8},{12,28},{28,12},{1,17},{... | collective-permute-start | bytes 6291464 | tf_op jit(solution)/shard_map/ppermute | solution.py:16
  226.3 46.5 %collective-permute-start.3 = (f32[2,2,1024,128]{3,2,1,0:T(8,128)}, f32[2,2,1024,128]{3,2,1,0:T(8,128)S(1)}, u32[]{:S(2)}, u32[]{:S(2)}) collective-permute-start(f32[2,2,1024,128]{3,2,1,0:T(8,128)} %get-tuple-element.11), channel_id=1, source_target_pairs={{0,8},{8,0},{4,12},{12,4},{16,24},{24,16},{20,28},{28,20},{1,9},{9... | collective-permute-start | bytes 6291464 | tf_op jit(solution)/shard_map/ppermute | solution.py:16
  228.0 89.8 %collective-permute-start.4 = (f32[2,2,1024,128]{3,2,1,0:T(8,128)}, f32[2,2,1024,128]{3,2,1,0:T(8,128)}, u32[]{:S(2)}, u32[]{:S(2)}) collective-permute-start(f32[2,2,1024,128]{3,2,1,0:T(8,128)} %get-tuple-element.10), channel_id=1, source_target_pairs={{0,8},{8,0},{4,12},{12,4},{16,24},{24,16},{20,28},{28,20},{1,9},{9... | collective-permute-start | bytes 6291464 | tf_op jit(solution)/shard_map/ppermute | solution.py:16
  272.8 1.4 copy-start.3
  323.3 45.1 %collective-permute-start.5 = (f32[2,2,1024,128]{3,2,1,0:T(8,128)S(1)}, f32[2,2,1024,128]{3,2,1,0:T(8,128)}, u32[]{:S(2)}, u32[]{:S(2)}) collective-permute-start(f32[2,2,1024,128]{3,2,1,0:T(8,128)S(1)} %get-tuple-element.8), channel_id=1, source_target_pairs={{0,4},{4,0},{8,12},{12,8},{16,20},{20,16},{24,28},{28,24},{1,5},{5... | collective-permute-start | bytes 6291464 | tf_op jit(solution)/shard_map/ppermute | solution.py:16
  323.6 89.8 %collective-permute-start.6 = (f32[2,2,1024,128]{3,2,1,0:T(8,128)}, f32[2,2,1024,128]{3,2,1,0:T(8,128)}, u32[]{:S(2)}, u32[]{:S(2)}) collective-permute-start(f32[2,2,1024,128]{3,2,1,0:T(8,128)} %get-tuple-element.9), channel_id=1, source_target_pairs={{0,4},{4,0},{8,12},{12,8},{16,20},{20,16},{24,28},{28,24},{1,5},{5... | collective-permute-start | bytes 6291464 | tf_op jit(solution)/shard_map/ppermute | solution.py:16
  465.1 21.7 %collective-permute-start.7 = (f32[2,1024,128]{2,1,0:T(8,128)S(1)}, f32[2,1024,128]{2,1,0:T(8,128)S(1)}, u32[]{:S(2)}, u32[]{:S(2)}) collective-permute-start(f32[2,1024,128]{2,1,0:T(8,128)S(1)} %get-tuple-element.23), channel_id=1, source_target_pairs={{0,4},{4,0},{8,12},{12,8},{16,20},{20,16},{24,28},{28,24},{1,5},{5... | collective-permute-start | bytes 3145736 | tf_op jit(solution)/shard_map/ppermute | solution.py:16
  465.2 44.2 %collective-permute-start.8 = (f32[2,1024,128]{2,1,0:T(8,128)S(1)}, f32[2,1024,128]{2,1,0:T(8,128)}, u32[]{:S(2)}, u32[]{:S(2)}) collective-permute-start(f32[2,1024,128]{2,1,0:T(8,128)S(1)} %get-tuple-element.22), channel_id=1, source_target_pairs={{0,4},{4,0},{8,12},{12,8},{16,20},{20,16},{24,28},{28,24},{1,5},{5... | collective-permute-start | bytes 3145736 | tf_op jit(solution)/shard_map/ppermute | solution.py:16
  486.8 1.0 copy-start.6
  512.2 24.0 %collective-permute-start.10 = (f32[2,1024,128]{2,1,0:T(8,128)S(1)}, f32[2,1024,128]{2,1,0:T(8,128)S(1)}, u32[]{:S(2)}, u32[]{:S(2)}) collective-permute-start(f32[2,1024,128]{2,1,0:T(8,128)S(1)} %get-tuple-element.16), channel_id=1, source_target_pairs={{0,8},{8,0},{4,12},{12,4},{16,24},{24,16},{20,28},{28,20},{1,9},{9... | collective-permute-start | bytes 3145736 | tf_op jit(solution)/shard_map/ppermute | solution.py:16
  515.9 42.9 %collective-permute-start.9 = (f32[2,1024,128]{2,1,0:T(8,128)}, f32[2,1024,128]{2,1,0:T(8,128)}, u32[]{:S(2)}, u32[]{:S(2)}) collective-permute-start(f32[2,1024,128]{2,1,0:T(8,128)} %get-tuple-element.17), channel_id=1, source_target_pairs={{0,8},{8,0},{4,12},{12,4},{16,24},{24,16},{20,28},{28,20},{1,9},{9... | collective-permute-start | bytes 3145736 | tf_op jit(solution)/shard_map/ppermute | solution.py:16
  536.2 1.0 copy-start.5
  561.0 95.2 %copy-start.8 = (f32[128]{0:T(128)S(1)}, f32[128]{0:T(128)}, u32[]{:S(2)}) copy-start(f32[128]{0:T(128)} %param.10) | copy-start | bytes 1540
  561.0 72.6 %collective-permute-start.11 = (f32[2,1024,128]{2,1,0:T(8,128)S(1)}, f32[2,1024,128]{2,1,0:T(8,128)S(1)}, u32[]{:S(2)}, u32[]{:S(2)}) collective-permute-start(f32[2,1024,128]{2,1,0:T(8,128)S(1)} %get-tuple-element.14), channel_id=1, source_target_pairs={{0,16},{16,0},{4,20},{20,4},{8,24},{24,8},{12,28},{28,12},{1,17},{... | collective-permute-start | bytes 3145736 | tf_op jit(solution)/shard_map/ppermute | solution.py:16
  565.2 91.0 %collective-permute-start.12 = (f32[2,1024,128]{2,1,0:T(8,128)S(1)}, f32[2,1024,128]{2,1,0:T(8,128)}, u32[]{:S(2)}, u32[]{:S(2)}) collective-permute-start(f32[2,1024,128]{2,1,0:T(8,128)S(1)} %get-tuple-element.15), channel_id=1, source_target_pairs={{0,16},{16,0},{4,20},{20,4},{8,24},{24,8},{12,28},{28,12},{1,17},{... | collective-permute-start | bytes 3145736 | tf_op jit(solution)/shard_map/ppermute | solution.py:16
  656.2 35.0 %copy-start.1 = (bf16[512,3,128]{2,0,1:T(8,128)(2,1)S(1)}, bf16[512,3,128]{2,0,1:T(8,128)(2,1)}, u32[]{:S(2)}) copy-start(bf16[512,3,128]{2,0,1:T(8,128)(2,1)} %param.7) | copy-start | bytes 1179652
Sparse Core Ops, SparseCore 0:
  8.9 19.3 all-gather.1
  659.8 29.6 reduce-scatter.1
where the time goes:
time: 704 us; the launch traced here: 699 us
  waiting for transfers between devices  580 us (82%)
  matrix products  47.3 us (7%)
  other arithmetic  26.2 us (4%)
  starting transfers between devices  19.4 us (3%)
  between operations  15.5 us (2%)
  local copies, waits for them, and re-layouts  10.4 us (1%)
    ppermute x12, waiting for transfers between devices, swapped(): return lax.ppermute(block, axis, route)  528 us
    reduce_scatter x1, waiting for transfers between devices, on_device(): lax.psum_scatter(terms, 'chan', scatter_dimension=1, tiled=True)  29.8 us
    all_gather x1, waiting for transfers between devices, on_device(): features = lax.all_gather(tokens, 'chan', axis=1, tiled=True)  21 us
    ppermute x12, starting transfers between devices, swapped(): return lax.ppermute(block, axis, route)  16.2 us
  transfers between devices with their start and end apart: 15, of which 15 were waited for; matrix products, arithmetic and copies ran while one was open for 0% of the time, Pallas kernels for 0%

commit v1 on v0

v1 whole, which is shorter than its diff:
```python
import functools
import math

import jax
import jax.numpy as jnp
import numpy as np
from jax import lax
from jax.experimental import pallas as pl
from jax.experimental.pallas import tpu as pltpu
from jax.sharding import PartitionSpec as P

MESH = pl.DeviceIdType.MESH
LANES = 128
RIM = 16
F32 = jnp.float32
BF16 = jnp.bfloat16


def split(values):
    high = values.astype(BF16)
    low = (values - high.astype(F32)).astype(BF16)
    return high, low


def split_table(table):
    table = np.asarray(table, np.float64)
    high = table.astype(np.float32).astype(BF16)
    low = (table - high.astype(np.float64)).astype(np.float32).astype(BF16)
    return high, low


def tables(total):
    first = total // LANES
    half = first // 2
    kept = half + 1
    padded = -(-kept // 16) * 16
    k1 = np.arange(padded)
    live = (k1 < kept).astype(np.float64)[:, None]
    n1 = np.arange(half)
    angle = 2.0 * math.pi / first * (k1[:, None] * n1[None, :] % first)
    outer = np.concatenate([np.cos(angle) * live, -np.sin(angle) * live], axis=0)
    outer_high, outer_low = split_table(outer)
    outer_table = np.concatenate([outer_high, outer_low], axis=1)
    n2 = np.arange(LANES)
    turn = 2.0 * math.pi / total * (k1[:, None] * n2[None, :] % total)
    turn_table = np.stack([np.cos(turn), -np.sin(turn)]).astype(np.float32)
    inner = 2.0 * math.pi / LANES * (n2[:, None] * n2[None, :] % LANES)
    cosine, sine = np.cos(inner), -np.sin(inner)
    ahead = np.block([[cosine, sine], [-sine, cosine]])
    ahead_table = np.stack(split_table(ahead))
    back_table = np.stack(split_table(ahead.T))
    weight = np.where((k1 == 0) | (k1 == half), 1.0, 2.0) * live[:, 0] / total
    close = np.concatenate([np.cos(angle).T * weight, -np.sin(angle).T * weight], axis=1)
    close_table = np.stack(split_table(close))
    return outer_table, turn_table, ahead_table, back_table, close_table


def dot(left, right):
    return jnp.dot(left, right, preferred_element_type=F32)


def dot3(left, table_ref):
    high, low = split(left)
    return dot(high, table_ref[0]) + (dot(low, table_ref[0]) + dot(high, table_ref[1]))


def kernel(
    shards, chans, chunks, group,
    tok, w_in, sfilt, lfilt, gain, w_out, outer_t, turn_t, ahead_t, back_t, close_t,
    out,
    tbuf, proj, rim_out, rim_in, keep, inner_s, stage, hs, hr, xs, xr, ys, yr,
    x32, h32, y32, cscr, gbuf, wbuf,
    tok_send, tok_recv, fwd_send, wo_send, wo_recv, rim_send, rim_recv,
    h_send, h_recv, x_send, x_recv, y_send, y_recv, g_send, g_recv, gf_send,
):
    seq = lax.axis_index("seq")
    chan = lax.axis_index("chan")
    count = tok.shape[0]
    blocks = count // LANES
    cd = LANES // shards
    half_rows = blocks // 2 * cd
    rows = count // chunks
    core_peer = chan + 1 - 2 * (chan % 2)
    x_peer = (chan + 2) % chans
    diag = (core_peer + 2) % chans
    others = (core_peer, x_peer, diag)

    barrier = pltpu.get_barrier_semaphore()
    for peer in others:
        pl.semaphore_signal(barrier, inc=1, device_id=(seq, peer), device_id_type=MESH)

    def greet(d, carry):
        peer = (seq + d) % shards
        pl.semaphore_signal(barrier, inc=1, device_id=(peer, chan), device_id_type=MESH)
        return carry

    lax.fori_loop(1, shards, greet, 0)
    pl.semaphore_wait(barrier, len(others) + shards - 1)

    def remote(src, dst, send, recv, device):
        return pltpu.make_async_remote_copy(
            src_ref=src, dst_ref=dst, send_sem=send, recv_sem=recv,
            device_id=device, device_id_type=MESH,
        )

    order = [chunks - 1] + list(range(chunks - 1))

    def tok_copy(k, slot, peer, owner):
        span = pl.ds(k * rows, rows)
        return remote(tok.at[span], tbuf.at[owner, span], tok_send.at[slot, k], tok_recv.at[owner, k], (seq, peer))

    def fwd_copy(k, owner):
        span = pl.ds(k * rows, rows)
        return remote(tbuf.at[owner, span], tbuf.at[owner, span], fwd_send.at[k], tok_recv.at[owner, k], (seq, core_peer))

    for k in order:
        tok_copy(k, 1, x_peer, chan).start()
        tok_copy(k, 0, core_peer, chan).start()

    def wo_copy(slot, peer, owner):
        columns = pl.ds(pl.multiple_of(peer * LANES, LANES), LANES)
        return remote(w_out.at[:, columns], wbuf.at[owner], wo_send.at[slot], wo_recv.at[owner], (seq, peer))

    def swap(src, dst, send, recv, half, peer, owner):
        span = pl.ds(half * half_rows, half_rows)
        return remote(src.at[peer, span], dst.at[owner, span], send.at[half, peer], recv.at[half, owner], (peer, chan))

    def swap_start(src, dst, send, recv, half):
        def one(d, carry):
            swap(src, dst, send, recv, half, (seq + d) % shards, seq).start()
            return carry
        lax.fori_loop(1, shards, one, 0)

    def swap_wait_recv(src, dst, send, recv, half):
        def one(d, carry):
            peer = (seq + d) % shards
            swap(src, dst, send, recv, half, peer, peer).wait_recv()
            return carry
        lax.fori_loop(1, shards, one, 0)

    def swap_wait_send(src, dst, send, recv, half):
        def one(d, carry):
            swap(src, dst, send, recv, half, (seq + d) % shards, seq).wait_send()
            return carry
        lax.fori_loop(1, shards, one, 0)

    def spread(values, block):
        turned = values.T
        for dest in range(shards):
            stage[dest, block * cd:(block + 1) * cd, :] = turned[dest * cd:(dest + 1) * cd, :]

    def pack(dst, half):
        span = slice(half * half_rows, (half + 1) * half_rows)
        dst[:, span, :] = stage[:, span, :].astype(BF16)

    for half in range(2):
        for block in range(half * blocks // 2, (half + 1) * blocks // 2):
            spread(lfilt[block * LANES:(block + 1) * LANES, :], block)
        pack(hs, half)
        swap_start(hs, hr, h_send, h_recv, half)
    hr[seq] = hs[seq]

    for slot, peer in enumerate(others):
        wo_copy(slot, peer, chan).start()
    wbuf[chan] = w_out[:, pl.ds(pl.multiple_of(chan * LANES, LANES), LANES)]
    tbuf[chan] = tok[...]

    def shorten(k):
        for g in range(3):
            lanes = slice(g * LANES, (g + 1) * LANES)
            base = RIM + k * rows
            value = (
                sfilt[0, g:g + 1, :] * proj[base:base + rows, lanes]
                + sfilt[1, g:g + 1, :] * proj[base - 1:base - 1 + rows, lanes]
                + sfilt[2, g:g + 1, :] * proj[base - 2:base - 2 + rows, lanes]
            )
            if g == 0:
                held = value
            elif g == 1:
                held = held * value
                inner_s[k * rows:(k + 1) * rows, :] = held
            else:
                keep[k * rows:(k + 1) * rows, :] = value
        for j in range(rows // LANES):
            spread(held[j * LANES:(j + 1) * LANES, :], k * (rows // LANES) + j)

    def rim_copy():
        return remote(rim_out, rim_in, rim_send, rim_recv, ((seq + 1) % shards, chan))

    for place, k in enumerate(order):
        tok_copy(k, 1, x_peer, x_peer).wait_recv()
        fwd_copy(k, x_peer).start()
        tok_copy(k, 0, core_peer, core_peer).wait_recv()
        tok_copy(k, 0, core_peer, diag).wait_recv()
        features = jnp.concatenate([tbuf[j, k * rows:(k + 1) * rows, :] for j in range(chans)], axis=1)
        projected = dot(features, w_in[...]).astype(BF16)
        proj[RIM + k * rows:RIM + (k + 1) * rows, :] = projected.astype(F32)
        if place == 0:
            rim_out[...] = projected[rows - RIM:, :]
            rim_copy().start()
        else:
            if place == 1:
                rim_copy().wait_recv()
                live = (seq > 0).astype(F32)
                proj[0:RIM, :] = rim_in[...].astype(F32) * live
            shorten(k)
            if (k + 1) * 2 == chunks:
                pack(xs, 0)
                swap_start(xs, xr, x_send, x_recv, 0)
    shorten(chunks - 1)
    pack(xs, 1)
    swap_start(xs, xr, x_send, x_recv, 1)
    xr[seq] = xs[seq]

    for half in range(2):
        swap_wait_recv(hs, hr, h_send, h_recv, half)
    h32[...] = hr[...].reshape(h32.shape).astype(F32)
    for half in range(2):
        swap_wait_recv(xs, xr, x_send, x_recv, half)
    x32[...] = xr[...].reshape(x32.shape).astype(F32)

    height = shards * blocks
    padded = turn_t.shape[1]

    def channels(i, carry):
        columns = []
        for ref in (x32, h32):
            for j in range(group):
                columns.append(ref[pl.ds(i * group + j, height, stride=cd), :].astype(BF16))
        signal = jnp.concatenate(columns, axis=1)
        signal = jnp.concatenate([signal, signal], axis=0)
        opened = dot(outer_t[...], signal)
        cosine, sine = turn_t[0], turn_t[1]
        turned = []
        for j in range(2 * group):
            real = opened[:padded, j * LANES:(j + 1) * LANES]
            imag = opened[padded:, j * LANES:(j + 1) * LANES]
            turned.append(jnp.concatenate([real * cosine - imag * sine, real * sine + imag * cosine], axis=1))
        spectra = dot3(jnp.concatenate(turned, axis=0), ahead_t)
        edge = group * padded
        xr_, xi_ = spectra[:edge, :LANES], spectra[:edge, LANES:]
        hr_, hi_ = spectra[edge:, :LANES], spectra[edge:, LANES:]
        product = jnp.concatenate([xr_ * hr_ - xi_ * hi_, xr_ * hi_ + xi_ * hr_], axis=1)
        back = dot3(product, back_t)
        sums = []
        for j in range(group):
            real = back[j * padded:(j + 1) * padded, :LANES]
            imag = back[j * padded:(j + 1) * padded, LANES:]
            sums.append(jnp.concatenate([real * cosine + imag * sine, imag * cosine - real * sine], axis=0))
        closing = jnp.concatenate(sums, axis=1)
        high, low = split(closing)
        conv = dot(close_t[0], high) + (dot(close_t[0], low) + dot(close_t[1], high))
        for j in range(group):
            y32[pl.ds(i * group + j, height, stride=cd), :] = conv[:, j * LANES:(j + 1) * LANES]
        return carry

    lax.fori_loop(0, cd // group, channels, 0)

    ys[...] = y32[...].astype(BF16).reshape(ys.shape)
    for half in range(2):
        swap_start(ys, yr, y_send, y_recv, half)
    yr[seq] = ys[seq]

    def gated_copy(half, slot, peer, owner):
        span = pl.ds(half * (count // 2), count // 2)
        return remote(gbuf.at[chan, span], gbuf.at[owner, span], g_send.at[slot, half], g_recv.at[owner, half], (seq, peer))

    def gated_fwd(half, owner):
        span = pl.ds(half * (count // 2), count // 2)
        return remote(gbuf.at[owner, span], gbuf.at[owner, span], gf_send.at[half], g_recv.at[owner, half], (seq, core_peer))

    for half in range(2):
        swap_wait_recv(ys, yr, y_send, y_recv, half)
        for src in range(shards):
            span = slice(half * half_rows, (half + 1) * half_rows)
            piece = yr[src, span, :].astype(F32)
            for j in range(blocks // 2):
                cscr[half * (blocks // 2) + j, src * cd:(src + 1) * cd, :] = piece[j * cd:(j + 1) * cd, :]
        for block in range(half * blocks // 2, (half + 1) * blocks // 2):
            span = slice(block * LANES, (block + 1) * LANES)
            conv = cscr[block].T
            gated = keep[span, :] * (conv + gain[...] * inner_s[span, :])
            gbuf[chan, span, :] = gated.astype(BF16)
        gated_copy(half, 1, x_peer, chan).start()
        gated_copy(half, 0, core_peer, chan).start()

    for slot, peer in enumerate(others):
        wo_copy(slot, peer, peer).wait_recv()
    weights = jnp.concatenate([wbuf[j] for j in range(chans)], axis=0)
    for half in range(2):
        gated_copy(half, 1, x_peer, x_peer).wait_recv()
        gated_fwd(half, x_peer).start()
    for half in range(2):
        gated_copy(half, 0, core_peer, core_peer).wait_recv()
        gated_copy(half, 0, core_peer, diag).wait_recv()
        span = slice(half * (count // 2), (half + 1) * (count // 2))
        whole = jnp.concatenate([gbuf[j, span, :] for j in range(chans)], axis=1)
        out[span, :] = dot(whole, weights).astype(BF16)

    for k in range(chunks):
        tok_copy(k, 1, x_peer, chan).wait_send()
        tok_copy(k, 0, core_peer, chan).wait_send()
        fwd_copy(k, x_peer).wait_send()
    for slot, peer in enumerate(others):
        wo_copy(slot, peer, chan).wait_send()
    rim_copy().wait_send()
    for half in range(2):
        swap_wait_send(hs, hr, h_send, h_recv, half)
        swap_wait_send(xs, xr, x_send, x_recv, half)
        swap_wait_send(ys, yr, y_send, y_recv, half)
        gated_copy(half, 1, x_peer, chan).wait_send()
        gated_copy(half, 0, core_peer, chan).wait_send()
        gated_fwd(half, x_peer).wait_send()


def on_device(shards, chans, tokens, w_in, short_filter, long_filter, skip_gain, w_out):
    count, width = tokens.shape
    length = shards * count
    blocks = count // LANES
    cd = width // shards
    chunks = 4
    group = min(cd, 4)
    consts = tables(2 * length)
    wide = 3 * width
    dma = pltpu.SemaphoreType.DMA
    swap_shape = (shards, blocks * cd, LANES)
    flat_shape = (shards * blocks * cd, LANES)
    vmem = pl.BlockSpec(memory_space=pltpu.VMEM)
    operands = (
        tokens, w_in.reshape(w_in.shape[0], wide), short_filter, long_filter,
        skip_gain.reshape(1, width), w_out,
    ) + tuple(jnp.asarray(c) for c in consts)
    return pl.pallas_call(
        functools.partial(kernel, shards, chans, chunks, group),
        out_shape=jax.ShapeDtypeStruct((count, width), BF16),
        in_specs=[vmem] * len(operands),
        out_specs=vmem,
        scratch_shapes=[
            pltpu.VMEM((chans, count, width), BF16),
            pltpu.VMEM((RIM + count, wide), F32),
            pltpu.VMEM((RIM, wide), BF16),
            pltpu.VMEM((RIM, wide), BF16),
            pltpu.VMEM((count, width), F32),
            pltpu.VMEM((count, width), F32),
            pltpu.VMEM(swap_shape, F32),
            pltpu.VMEM(swap_shape, BF16),
            pltpu.VMEM(swap_shape, BF16),
            pltpu.VMEM(swap_shape, BF16),
            pltpu.VMEM(swap_shape, BF16),
            pltpu.VMEM(swap_shape, BF16),
            pltpu.VMEM(swap_shape, BF16),
            pltpu.VMEM(flat_shape, F32),
            pltpu.VMEM(flat_shape, F32),
            pltpu.VMEM(flat_shape, F32),
            pltpu.VMEM((blocks, LANES, LANES), F32),
            pltpu.VMEM((chans, count, width), BF16),
            pltpu.VMEM((chans, width, LANES), BF16),
            dma((2, chunks)), dma((chans, chunks)), dma((chunks,)),
            dma((3,)), dma((chans,)), dma, dma,
            dma((2, shards)), dma((2, shards)),
            dma((2, shards)), dma((2, shards)),
            dma((2, shards)), dma((2, shards)),
            dma((2, 2)), dma((chans, 2)), dma((2,)),
        ],
        compiler_params=pltpu.CompilerParams(
            collective_id=0, has_side_effects=True, vmem_limit_bytes=48 * 1024 * 1024
        ),
        cost_estimate=pl.CostEstimate(flops=4 * 10**9, bytes_accessed=4 * 10**6, transcendentals=0),
    )(*operands)


def solution(mesh):
    shards, chans = mesh.shape["seq"], mesh.shape["chan"]
    return jax.shard_map(
        functools.partial(on_device, shards, chans),
        mesh=mesh,
        in_specs=(
            P("seq", "chan"),
            P(None, None, "chan"),
            P(None, None, "chan"),
            P("seq", "chan"),
            P("chan"),
            P("chan", None),
        ),
        out_specs=P("seq", "chan"),
        check_vma=False,
    )
```

time: 704 us -> 46.9 us (0.07)
  waiting for transfers between devices: 580 us -> 0 us
  matrix products: 47.3 us -> 0 us
  Pallas kernels: 0 us -> 42.8 us
  other arithmetic: 26.2 us -> 0 us
  starting transfers between devices: 19.4 us -> 0 us
  between operations: 15.5 us -> 0.12 us
    ppermute x13 -> x0, waiting for transfers between devices: 528 us -> none  [the longest x12 528 us: swapped(): return lax.ppermute(block, axis, route)]
    dot_general x18 -> x0, matrix products: 47.3 us -> none  [the longest x4 10.9 us: table_product(): cos_imag = jnp.einsum(form, cosine, imag_part, precision=highest)]
    pallas_call x0 -> x1, Pallas kernels: none -> 42.8 us  [on_device(): pl.pallas_call(functools.partial(kernel, shards, chans, chunks, group), o...]
    reduce_scatter x1 -> x0, waiting for transfers between devices: 29.8 us -> none  [on_device(): lax.psum_scatter(terms, 'chan', scatter_dimension=1, tiled=True)]
    all_gather x1 -> x0, waiting for transfers between devices: 21 us -> none  [on_device(): features = lax.all_gather(tokens, 'chan', axis=1, tiled=True)]
    ppermute x13 -> x0, starting transfers between devices: 19.3 us -> none  [the longest x12 16.2 us: swapped(): return lax.ppermute(block, axis, route)]
    add x7 -> x0, other arithmetic: 12.7 us -> none  [the longest x5 12.2 us: rotate(): real_part * sine + imag_part * cosine]
    sub x4 -> x0, other arithmetic: 9.2 us -> none  [the longest x3 8.98 us: rotate(): real_part * cosine - imag_part * sine]
  transfers between devices with their start and end apart: 15 -> 0, of which waited for: 15 -> 0; matrix products, arithmetic and copies ran while one was open for 0% -> 0% of each run, Pallas kernels for 0% -> 0%
where the time goes in v1:
time: 46.9 us; the launch traced here: 46.7 us
  Pallas kernels  42.8 us (91%)
  local copies, waits for them, and re-layouts  3.83 us (8%)
    pallas_call x1, Pallas kernels, on_device(): pl.pallas_call(functools.partial(kernel, shards, chans, chunks, group), o...  42.8 us
    unnamed x22, local copies, waits for them, and re-layouts  3.62 us

profile of v1, /device:TPU:1, one launch (start us, length us, event | category | flops | bytes accessed | tf_op | source)
XLA Modules:
  0.0 46.7 jit_solution(13887176132846503486)
XLA Ops:
  0.0 0.0 copy-start.2
  0.0 0.0 copy-start.3
  0.0 0.0 copy-start.5
  0.0 0.0 copy-start.6
  0.0 0.0 copy-start.7
  0.0 0.0 copy-start.9
  0.0 1.2 %copy.13 = bf16[512,3,128]{0,2,1:T(8,128)(2,1)S(1)} copy(bf16[512,3,128]{2,0,1:T(8,128)(2,1)} %param.12) | data formatting | bytes 786432 | tf_op args[1]
  1.3 0.0 copy-start
  1.3 0.0 copy-start.1
  1.3 0.0 copy-start.4
  1.3 0.2 copy.14.w_in
  1.5 0.0 copy-done.2
  1.5 0.0 copy-done.3
  1.6 0.0 copy-done.5
  1.6 0.0 copy-done.6
  1.6 0.0 copy-done.7
  1.6 0.0 copy-done.9
  1.6 0.7 %copy-done = f32[1024,128]{1,0:T(8,128)S(1)} copy-done((f32[1024,128]{1,0:T(8,128)S(1)}, f32[1024,128]{1,0:T(8,128)}, u32[]{:S(2)}) %copy-start) | copy-done | bytes 524312
  2.3 0.1 copy-done.1
  2.4 0.0 copy-done.4
  2.4 0.0 copy-start.8
  2.4 0.8 %copy-done.8 = bf16[2,64,160]{2,1,0:T(8,128)(2,1)S(1)} copy-done((bf16[2,64,160]{2,1,0:T(8,128)(2,1)S(1)}, bf16[2,64,160]{2,1,0:T(8,128)(2,1)}, u32[]{:S(2)}) %copy-start.8) | copy-done | bytes 40984
  3.2 42.8 %shard_map.109 = bf16[1024,128]{1,0:T(8,128)(2,1)S(1)} custom-call(bf16[1024,128]{1,0:T(8,128)(2,1)S(1)} %copy-done.1, bf16[512,384]{1,0:T(8,128)(2,1)S(1)} %copy.14.w_in, f32[3,3,128]{2,1,0:T(4,128)S(1)} %copy-done.3, f32[1024,128]{1,0:T(8,128)S(1)} %copy-done, f32[1,128]{1,0:T(1,128)S(1)} %bitcast.2, bf16[128,512]{1,0:T(8,128)(2,1)S(1)} %copy-done.2, ...), custom_call_target="tpu_custom_call" | custom-call | flops 4000000000 | bytes 4000000 | tf_op jit(solution)/shard_map/pallas_call | solution.py:333
  46.0 0.7 %copy.16 = bf16[1024,128]{1,0:T(8,128)(2,1)} copy(bf16[1024,128]{1,0:T(8,128)(2,1)S(1)} %shard_map.109) | data formatting | bytes 524288
Async XLA Ops:
  0.0 1.5 %copy-start.2 = (bf16[128,512]{1,0:T(8,128)(2,1)S(1)}, bf16[128,512]{1,0:T(8,128)(2,1)}, u32[]{:S(2)}) copy-start(bf16[128,512]{1,0:T(8,128)(2,1)} %w_out.1) | copy-start | bytes 393220
  0.0 1.5 %copy-start.3 = (f32[3,3,128]{2,1,0:T(4,128)S(1)}, f32[3,3,128]{2,1,0:T(4,128)}, u32[]{:S(2)}) copy-start(f32[3,3,128]{2,1,0:T(4,128)} %sfilt.1) | copy-start | bytes 13828
  0.0 1.6 %copy-start.5 = (bf16[2,256,256]{2,1,0:T(8,128)(2,1)S(1)}, bf16[2,256,256]{2,1,0:T(8,128)(2,1)}, u32[]{:S(2)}) copy-start(bf16[2,256,256]{2,1,0:T(8,128)(2,1)} %constant.13.clone.back_t) | copy-start | bytes 786436
  0.0 1.6 %copy-start.6 = (bf16[2,256,256]{2,1,0:T(8,128)(2,1)S(1)}, bf16[2,256,256]{2,1,0:T(8,128)(2,1)}, u32[]{:S(2)}) copy-start(bf16[2,256,256]{2,1,0:T(8,128)(2,1)} %constant.12.clone.ahead_t) | copy-start | bytes 786436
  0.0 1.6 %copy-start.7 = (f32[2,80,128]{2,1,0:T(8,128)S(1)}, f32[2,80,128]{2,1,0:T(8,128)}, u32[]{:S(2)}) copy-start(f32[2,80,128]{2,1,0:T(8,128)} %constant.11.clone.turn_t) | copy-start | bytes 245764
  0.0 1.6 %copy-start.9 = (bf16[160,128]{1,0:T(8,128)(2,1)S(1)}, bf16[160,128]{1,0:T(8,128)(2,1)}, u32[]{:S(2)}) copy-start(bf16[160,128]{1,0:T(8,128)(2,1)} %constant.10.clone.outer_t) | copy-start | bytes 122884
  1.3 1.0 %copy-start = (f32[1024,128]{1,0:T(8,128)S(1)}, f32[1024,128]{1,0:T(8,128)}, u32[]{:S(2)}) copy-start(f32[1024,128]{1,0:T(8,128)} %lfilt.1) | copy-start | bytes 1572868
  1.3 1.1 %copy-start.1 = (bf16[1024,128]{1,0:T(8,128)(2,1)S(1)}, bf16[1024,128]{1,0:T(8,128)(2,1)}, u32[]{:S(2)}) copy-start(bf16[1024,128]{1,0:T(8,128)(2,1)} %tok.1) | copy-start | bytes 786436
  1.3 1.1 %copy-start.4 = (f32[128]{0:T(128)S(1)}, f32[128]{0:T(128)}, u32[]{:S(2)}) copy-start(f32[128]{0:T(128)} %param.15) | copy-start | bytes 1540
  2.4 0.8 %copy-start.8 = (bf16[2,64,160]{2,1,0:T(8,128)(2,1)S(1)}, bf16[2,64,160]{2,1,0:T(8,128)(2,1)}, u32[]{:S(2)}) copy-start(bf16[2,64,160]{2,1,0:T(8,128)(2,1)} %constant.14.clone.close_t) | copy-start | bytes 122884

commit v2 on v1

v2 whole, which is shorter than its diff:
```python
import functools
import math

import jax
import jax.numpy as jnp
import numpy as np
from jax import lax
from jax.experimental import pallas as pl
from jax.experimental.pallas import tpu as pltpu
from jax.sharding import PartitionSpec as P

MESH = pl.DeviceIdType.MESH
LANES = 128
RIM = 16
F32 = jnp.float32
BF16 = jnp.bfloat16


def split(values):
    high = values.astype(BF16)
    low = (values - high.astype(F32)).astype(BF16)
    return high, low


def split_table(table):
    table = np.asarray(table, np.float64)
    high = table.astype(np.float32).astype(BF16)
    low = (table - high.astype(np.float64)).astype(np.float32).astype(BF16)
    return high, low


def tables(total):
    first = total // LANES
    half = first // 2
    kept = half + 1
    padded = -(-kept // 16) * 16
    k1 = np.arange(padded)
    live = (k1 < kept).astype(np.float64)[:, None]
    n1 = np.arange(half)
    angle = 2.0 * math.pi / first * (k1[:, None] * n1[None, :] % first)
    outer = np.concatenate([np.cos(angle) * live, -np.sin(angle) * live], axis=0)
    outer_table = np.concatenate(split_table(outer), axis=1).astype(np.float32)
    n2 = np.arange(LANES)
    turn = 2.0 * math.pi / total * (k1[:, None] * n2[None, :] % total)
    turn_table = np.stack([np.cos(turn), -np.sin(turn)]).astype(np.float32)
    inner = 2.0 * math.pi / LANES * (n2[:, None] * n2[None, :] % LANES)
    cosine, sine = np.cos(inner), -np.sin(inner)
    ahead = np.block([[cosine, sine], [-sine, cosine]])
    ahead_table = ahead.astype(np.float32)
    back_table = ahead.T.astype(np.float32)
    weight = np.where((k1 == 0) | (k1 == half), 1.0, 2.0) * live[:, 0] / total
    close = np.concatenate([np.cos(angle).T * weight, -np.sin(angle).T * weight], axis=1)
    close_table = close.astype(np.float32)
    return outer_table, turn_table, ahead_table, back_table, close_table


def dot(left, right):
    return jnp.dot(left, right, preferred_element_type=F32)


def dot3(left, table_ref):
    high, low = split(left)
    return dot(high, table_ref[0]) + (dot(low, table_ref[0]) + dot(high, table_ref[1]))


def kernel(
    shards, chans, chunks, parts, group,
    tok, w_in, sfilt_a, lfilt_a, gain_a, w_out, outer_a, turn_a, ahead_a, back_a, close_a,
    out,
    tbuf, tmini, w, sfilt, lfilt, gain, outer_f, turn_t, ahead_f, back_f, close_f,
    outer_t, ahead_t, back_t, close_t,
    proj, rim_out, rim_in, keep, keep_t, skip_t, stage, hs, hr, xs, xr, ys, yr,
    x32, h32, hspec, y32, c32, gbuf, wbuf, w32, wt, acc,
    local, tok_send, tok_recv, fwd_send, wo_send, wo_recv, rim_send, rim_recv,
    h_send, h_recv, x_send, x_recv, y_send, y_recv, g_send, g_recv, gf_send,
):
    seq = lax.axis_index("seq")
    chan = lax.axis_index("chan")
    count = tok.shape[0]
    blocks = count // LANES
    cd = LANES // shards
    groups = cd // group
    rows = count // chunks
    core_peer = chan + 1 - 2 * (chan % 2)
    x_peer = (chan + 2) % chans
    diag = (core_peer + 2) % chans
    others = (core_peer, x_peer, diag)

    own_columns = pl.ds(pl.multiple_of(chan * LANES, LANES), LANES)
    loads = [(lfilt_a, lfilt), (tok, tbuf.at[chan]), (tok.at[pl.ds(count - RIM, RIM)], tmini.at[chan])]
    loads += [(w_in.at[g], w.at[:, pl.ds(g * LANES, LANES)]) for g in range(3)]
    loads += [(sfilt_a, sfilt), (gain_a, gain), (w_out.at[:, own_columns], wbuf.at[chan])]
    loads += [(outer_a, outer_f), (turn_a, turn_t), (ahead_a, ahead_f), (back_a, back_f), (close_a, close_f)]
    copies = [pltpu.make_async_copy(src, dst, local.at[i]) for i, (src, dst) in enumerate(loads)]
    for copy in copies:
        copy.start()

    barrier = pltpu.get_barrier_semaphore()
    for peer in others:
        pl.semaphore_signal(barrier, inc=1, device_id=(seq, peer), device_id_type=MESH)

    def greet(d, carry):
        peer = (seq + d) % shards
        pl.semaphore_signal(barrier, inc=1, device_id=(peer, chan), device_id_type=MESH)
        return carry

    lax.fori_loop(1, shards, greet, 0)
    pl.semaphore_wait(barrier, len(others) + shards - 1)

    def remote(src, dst, send, recv, device):
        return pltpu.make_async_remote_copy(
            src_ref=src, dst_ref=dst, send_sem=send, recv_sem=recv,
            device_id=device, device_id_type=MESH,
        )

    def landing(k, owner):
        if k == 0:
            return tmini.at[owner]
        return tbuf.at[owner, pl.ds((k - 1) * rows, rows)]

    def tok_copy(k, slot, peer, owner):
        span = pl.ds(count - RIM, RIM) if k == 0 else pl.ds((k - 1) * rows, rows)
        return remote(tok.at[span], landing(k, owner), tok_send.at[slot, k], tok_recv.at[owner, k], (seq, peer))

    def fwd_copy(k, owner):
        return remote(landing(k, owner), landing(k, owner), fwd_send.at[k], tok_recv.at[owner, k], (seq, core_peer))

    for k in range(chunks + 1):
        tok_copy(k, 1, x_peer, chan).start()
        tok_copy(k, 0, core_peer, chan).start()

    def wo_copy(slot, peer, owner):
        columns = pl.ds(pl.multiple_of(peer * LANES, LANES), LANES)
        return remote(w_out.at[:, columns], wbuf.at[owner], wo_send.at[slot], wo_recv.at[owner], (seq, peer))

    def swap(src, dst, send, recv, part, span, peer, owner):
        return remote(src.at[peer, span], dst.at[owner, span], send.at[part, peer], recv.at[part, owner], (peer, chan))

    def swap_all(action, src, dst, send, recv, part, span):
        def one(d, carry):
            peer = (seq + d) % shards
            if action == "start":
                swap(src, dst, send, recv, part, span, peer, seq).start()
            elif action == "recv":
                swap(src, dst, send, recv, part, span, peer, peer).wait_recv()
            else:
                swap(src, dst, send, recv, part, span, peer, seq).wait_send()
            return carry
        lax.fori_loop(1, shards, one, 0)

    def h_swap(action, half):
        size = blocks // 2 * cd
        swap_all(action, hs, hr, h_send, h_recv, half, pl.ds(half * size, size))

    def x_swap(action, part):
        size = blocks // parts * cd
        swap_all(action, xs, xr, x_send, x_recv, part, pl.ds(part * size, size))

    def y_swap(action, g):
        swap_all(action, ys.at[g], yr.at[g], y_send, y_recv, g, pl.ds(0, group * blocks))

    def spread(turned, block):
        for dest in range(shards):
            stage[dest, block * cd:(block + 1) * cd, :] = turned[dest * cd:(dest + 1) * cd, :]

    def pack(dst, part, pieces):
        size = blocks // pieces * cd
        span = slice(part * size, (part + 1) * size)
        dst[:, span, :] = stage[:, span, :].astype(BF16)

    copies[0].wait()
    for half in range(2):
        for block in range(half * blocks // 2, (half + 1) * blocks // 2):
            spread(lfilt[block * LANES:(block + 1) * LANES, :].T, block)
        pack(hs, half, 2)
        h_swap("start", half)
    hr[seq] = hs[seq]
    for slot, peer in enumerate(others):
        wo_copy(slot, peer, chan).start()
    for copy in copies[1:]:
        copy.wait()
    gain_rows = jnp.broadcast_to(gain[...], (LANES, LANES)).T

    def shorten(k):
        for g in range(3):
            lanes = slice(g * LANES, (g + 1) * LANES)
            base = RIM + k * rows
            value = (
                sfilt[0, g:g + 1, :] * proj[base:base + rows, lanes]
                + sfilt[1, g:g + 1, :] * proj[base - 1:base - 1 + rows, lanes]
                + sfilt[2, g:g + 1, :] * proj[base - 2:base - 2 + rows, lanes]
            )
            if g == 0:
                held = value
            elif g == 1:
                held = held * value
            else:
                keep[k * rows:(k + 1) * rows, :] = value
        for j in range(rows // LANES):
            block = k * (rows // LANES) + j
            turned = held[j * LANES:(j + 1) * LANES, :].T
            spread(turned, block)
            skip_t[block * LANES:(block + 1) * LANES, :] = turned * gain_rows

    def rim_copy():
        return remote(rim_out, rim_in, rim_send, rim_recv, ((seq + 1) % shards, chan))

    def take(k):
        tok_copy(k, 1, x_peer, x_peer).wait_recv()
        fwd_copy(k, x_peer).start()
        tok_copy(k, 0, core_peer, core_peer).wait_recv()
        tok_copy(k, 0, core_peer, diag).wait_recv()

    take(0)
    tail = jnp.concatenate([tmini[j] for j in range(chans)], axis=1)
    rim_out[...] = dot(tail, w[...]).astype(BF16)
    rim_copy().start()
    outer_t[...] = outer_f[...].astype(BF16)
    for table, ref in ((ahead_f, ahead_t), (back_f, back_t), (close_f, close_t)):
        high, low = split(table[...])
        ref[0] = high
        ref[1] = low
    for k in range(chunks):
        take(k + 1)
        features = jnp.concatenate([tbuf[j, k * rows:(k + 1) * rows, :] for j in range(chans)], axis=1)
        projected = dot(features, w[...]).astype(BF16)
        proj[RIM + k * rows:RIM + (k + 1) * rows, :] = projected.astype(F32)
        if k == 0:
            rim_copy().wait_recv()
            live = (seq > 0).astype(F32)
            proj[0:RIM, :] = rim_in[...].astype(F32) * live
        shorten(k)
        if (k + 1) * parts % chunks == 0:
            part = (k + 1) * parts // chunks - 1
            pack(xs, part, parts)
            x_swap("start", part)
    xr[seq] = xs[seq]

    height = shards * blocks
    padded = turn_t.shape[1]
    edge = group * padded

    def spectrum(ref, g):
        columns = [ref[pl.ds(g * group + j, height, stride=cd), :].astype(BF16) for j in range(group)]
        signal = jnp.concatenate(columns, axis=1)
        signal = jnp.concatenate([signal, signal], axis=0)
        opened = dot(outer_t[...], signal)
        cosine, sine = turn_t[0], turn_t[1]
        turned = []
        for j in range(group):
            real = opened[:padded, j * LANES:(j + 1) * LANES]
            imag = opened[padded:, j * LANES:(j + 1) * LANES]
            turned.append(jnp.concatenate([real * cosine - imag * sine, real * sine + imag * cosine], axis=1))
        return dot3(jnp.concatenate(turned, axis=0), ahead_t)

    for half in range(2):
        h_swap("recv", half)
    h32[...] = hr[...].reshape(h32.shape).astype(F32)
    for g in range(groups):
        hspec[g] = spectrum(h32, g)
    for block in range(blocks):
        span = slice(block * LANES, (block + 1) * LANES)
        keep_t[span, :] = keep[span, :].T
    for slot, peer in enumerate(others):
        wo_copy(slot, peer, peer).wait_recv()
    for j in range(chans):
        w32[...] = wbuf[j].astype(F32)
        for g in range(groups):
            picked = [w32[pl.ds(g * group + c, shards, stride=cd), :] for c in range(group)]
            wt[g, j] = jnp.concatenate(picked, axis=0).astype(BF16)

    for part in range(parts):
        x_swap("recv", part)
    x32[...] = xr[...].reshape(x32.shape).astype(F32)

    def convolve(g):
        spectra = spectrum(x32, g)
        xr_, xi_ = spectra[:, :LANES], spectra[:, LANES:]
        hr_, hi_ = hspec[g, :, :LANES], hspec[g, :, LANES:]
        product = jnp.concatenate([xr_ * hr_ - xi_ * hi_, xr_ * hi_ + xi_ * hr_], axis=1)
        back = dot3(product, back_t)
        cosine, sine = turn_t[0], turn_t[1]
        sums = []
        for j in range(group):
            real = back[j * padded:(j + 1) * padded, :LANES]
            imag = back[j * padded:(j + 1) * padded, LANES:]
            sums.append(jnp.concatenate([real * cosine + imag * sine, imag * cosine - real * sine], axis=0))
        high, low = split(jnp.concatenate(sums, axis=1))
        conv = dot(close_t[0], high) + (dot(close_t[0], low) + dot(close_t[1], high))
        for j in range(group):
            y32[:, j * blocks:(j + 1) * blocks, :] = conv[:, j * LANES:(j + 1) * LANES].reshape(shards, blocks, LANES)
        ys[g] = y32[...].astype(BF16)
        y_swap("start", g)
        yr[g, seq] = ys[g, seq]

    def gated_copy(g, slot, peer, owner):
        return remote(gbuf.at[chan, g], gbuf.at[owner, g], g_send.at[slot, g], g_recv.at[owner, g], (seq, peer))

    def gated_fwd(g, owner):
        return remote(gbuf.at[owner, g], gbuf.at[owner, g], gf_send.at[g], g_recv.at[owner, g], (seq, core_peer))

    def gate(g):
        y_swap("recv", g)
        c32[...] = yr[g].reshape(c32.shape).astype(F32)
        for block in range(blocks):
            pieces = []
            for c in range(group):
                conv = c32[pl.ds(c * blocks + block, shards, stride=group * blocks), :]
                at = pl.ds(block * LANES + g * group + c, shards, stride=cd)
                pieces.append(keep_t[at, :] * (conv + skip_t[at, :]))
            gbuf[chan, g, :, block * LANES:(block + 1) * LANES] = jnp.concatenate(pieces, axis=0).astype(BF16)
        gated_copy(g, 1, x_peer, chan).start()
        gated_copy(g, 0, core_peer, chan).start()

    def forward(g):
        gated_copy(g, 1, x_peer, x_peer).wait_recv()
        gated_fwd(g, x_peer).start()

    def mix(g):
        gated_copy(g, 0, core_peer, core_peer).wait_recv()
        gated_copy(g, 0, core_peer, diag).wait_recv()
        whole = jnp.concatenate([gbuf[j, g] for j in range(chans)], axis=0)
        weights = jnp.concatenate([wt[g, j] for j in range(chans)], axis=0)
        part = dot(weights.astype(F32).T.astype(BF16), whole)
        if g > 0:
            part = part + acc[...]
        if g < groups - 1:
            acc[...] = part
        else:
            for block in range(blocks):
                span = slice(block * LANES, (block + 1) * LANES)
                out[span, :] = part[:, span].T.astype(BF16)

    for g in range(groups):
        convolve(g)
        if g >= 1:
            gate(g - 1)
        if g >= 2:
            forward(g - 2)
    gate(groups - 1)
    for g in range(max(groups - 2, 0), groups - 1):
        forward(g)
    for g in range(groups - 2):
        mix(g)
    forward(groups - 1)
    for g in range(max(groups - 2, 0), groups):
        mix(g)

    for k in range(chunks + 1):
        tok_copy(k, 1, x_peer, chan).wait_send()
        tok_copy(k, 0, core_peer, chan).wait_send()
        fwd_copy(k, x_peer).wait_send()
    for slot, peer in enumerate(others):
        wo_copy(slot, peer, chan).wait_send()
    rim_copy().wait_send()
    for half in range(2):
        h_swap("send", half)
    for part in range(parts):
        x_swap("send", part)
    for g in range(groups):
        y_swap("send", g)
        gated_copy(g, 1, x_peer, chan).wait_send()
        gated_copy(g, 0, core_peer, chan).wait_send()
        gated_fwd(g, x_peer).wait_send()


def on_device(shards, chans, tokens, w_in, short_filter, long_filter, skip_gain, w_out):
    count, width = tokens.shape
    length = shards * count
    blocks = count // LANES
    cd = width // shards
    chunks = 4
    parts = 4 if blocks // 4 * cd % 16 == 0 else 2
    group = min(cd, 4)
    groups = cd // group
    consts = tables(2 * length)
    outer, turn, ahead, back, close = consts
    wide = 3 * width
    inputs = w_in.shape[0]
    dma = pltpu.SemaphoreType.DMA
    vmem = pltpu.VMEM
    swap_shape = (shards, blocks * cd, LANES)
    flat_shape = (shards * blocks * cd, LANES)
    back_shape = (groups, shards, group * blocks, LANES)
    operands = (
        tokens, w_in.transpose(1, 0, 2), short_filter, long_filter,
        skip_gain.reshape(1, width), w_out,
    ) + tuple(jnp.asarray(c) for c in consts)
    return pl.pallas_call(
        functools.partial(kernel, shards, chans, chunks, parts, group),
        out_shape=jax.ShapeDtypeStruct((count, width), BF16),
        in_specs=[pl.BlockSpec(memory_space=pl.ANY)] * len(operands),
        out_specs=pl.BlockSpec(memory_space=vmem),
        scratch_shapes=[
            vmem((chans, count, width), BF16),
            vmem((chans, RIM, width), BF16),
            vmem((inputs, wide), BF16),
            vmem(short_filter.shape, F32),
            vmem((count, width), F32),
            vmem((1, width), F32),
        ] + [vmem(c.shape, F32) for c in consts] + [
            vmem(outer.shape, BF16),
            vmem((2,) + ahead.shape, BF16),
            vmem((2,) + back.shape, BF16),
            vmem((2,) + close.shape, BF16),
            vmem((RIM + count, wide), F32),
            vmem((RIM, wide), BF16),
            vmem((RIM, wide), BF16),
            vmem((count, width), F32),
            vmem((blocks * LANES, LANES), F32),
            vmem((blocks * LANES, LANES), F32),
            vmem(swap_shape, F32),
            vmem(swap_shape, BF16),
            vmem(swap_shape, BF16),
            vmem(swap_shape, BF16),
            vmem(swap_shape, BF16),
            vmem(back_shape, BF16),
            vmem(back_shape, BF16),
            vmem(flat_shape, F32),
            vmem(flat_shape, F32),
            vmem((groups, group * turn.shape[1], 2 * LANES), F32),
            vmem(back_shape[1:], F32),
            vmem((shards * group * blocks, LANES), F32),
            vmem((chans, groups, group * shards, count), BF16),
            vmem((chans, width, LANES), BF16),
            vmem((width, LANES), F32),
            vmem((groups, chans, group * shards, LANES), BF16),
            vmem((LANES, count), F32),
            dma((14,)),
            dma((2, chunks + 1)), dma((chans, chunks + 1)), dma((chunks + 1,)),
            dma((3,)), dma((chans,)), dma, dma,
            dma((2, shards)), dma((2, shards)),
            dma((parts, shards)), dma((parts, shards)),
            dma((groups, shards)), dma((groups, shards)),
            dma((2, groups)), dma((chans, groups)), dma((groups,)),
        ],
        compiler_params=pltpu.CompilerParams(
            collective_id=0, has_side_effects=True, vmem_limit_bytes=56 * 1024 * 1024
        ),
        cost_estimate=pl.CostEstimate(flops=4 * 10**9, bytes_accessed=4 * 10**6, transcendentals=0),
    )(*operands)


def solution(mesh):
    shards, chans = mesh.shape["seq"], mesh.shape["chan"]
    return jax.shard_map(
        functools.partial(on_device, shards, chans),
        mesh=mesh,
        in_specs=(
            P("seq", "chan"),
            P(None, None, "chan"),
            P(None, None, "chan"),
            P("seq", "chan"),
            P("chan"),
            P("chan", None),
        ),
        out_specs=P("seq", "chan"),
        check_vma=False,
    )
```

time: 46.9 us -> 45.6 us (0.972)
  local copies, waits for them, and re-layouts: 3.83 us -> 1.67 us
  Pallas kernels: 42.8 us -> 43.8 us
    unnamed x22 -> x1, local copies, waits for them, and re-layouts: 3.62 us -> 1.67 us
    pallas_call x1, Pallas kernels: 42.8 us -> 43.8 us  [on_device(): pl.pallas_call(functools.partial(kernel, shards, chans, chunks, parts, gr...]
where the time goes in v2:
time: 45.6 us; the launch traced here: 45.5 us
  Pallas kernels  43.8 us (96%)
  local copies, waits for them, and re-layouts  1.67 us (4%)
    pallas_call x1, Pallas kernels, on_device(): pl.pallas_call(functools.partial(kernel, shards, chans, chunks, parts, gr...  43.8 us
    unnamed x1, local copies, waits for them, and re-layouts  1.67 us

profile of v2, /device:TPU:1, one launch (start us, length us, event | category | flops | bytes accessed | tf_op | source)
XLA Modules:
  0.0 45.5 jit_solution(10941145354200538855)
XLA Ops:
  0.0 43.8 %shard_map.109 = bf16[1024,128]{1,0:T(8,128)(2,1)} custom-call(bf16[1024,128]{1,0:T(8,128)(2,1)} %tok.1, bf16[3,512,128]{2,1,0:T(8,128)(2,1)} %bitcast.2, f32[3,3,128]{2,1,0:T(4,128)} %sfilt_a.1, f32[1024,128]{1,0:T(8,128)} %lfilt_a.1, f32[1,128]{1,0:T(1,128)} %bitcast.3, bf16[128,512]{1,0:T(8,128)(2,1)} %w_out.1, f32[160,128]{1,0:T(8,128)} %constant.10.clone.outer_a, ...), custom_call_target="tpu_custom_call" | custom-call | flops 4000000000 | bytes 4000000 | tf_op jit(solution)/shard_map/pallas_call | solution.py:389
  43.8 1.7 %copy.13 = bf16[1024,128]{1,0:T(8,128)(2,1)} copy(bf16[1024,128]{1,0:T(8,128)(2,1)} %shard_map.109) | data formatting | bytes 524288

commit v3 on v2

--- a/solution.py
+++ b/solution.py
@@ -58,9 +58,9 @@
     return jnp.dot(left, right, preferred_element_type=F32)
 
 
-def dot3(left, table_ref):
-    high, low = split(left)
-    return dot(high, table_ref[0]) + (dot(low, table_ref[0]) + dot(high, table_ref[1]))
+def dot2(left, table_ref):
+    rounded = left.astype(BF16)
+    return dot(rounded, table_ref[0]) + dot(rounded, table_ref[1])
 
 
 def kernel(
@@ -70,7 +70,7 @@
     tbuf, tmini, w, sfilt, lfilt, gain, outer_f, turn_t, ahead_f, back_f, close_f,
     outer_t, ahead_t, back_t, close_t,
     proj, rim_out, rim_in, keep, keep_t, skip_t, stage, hs, hr, xs, xr, ys, yr,
-    x32, h32, hspec, y32, c32, gbuf, wbuf, w32, wt, acc,
+    x32, h32, hspec, y32, c32, gbuf, wbuf, w32, w_rows, wt, acc, gain_rows,
     local, tok_send, tok_recv, fwd_send, wo_send, wo_recv, rim_send, rim_recv,
     h_send, h_recv, x_send, x_recv, y_send, y_recv, g_send, g_recv, gf_send,
 ):
@@ -85,6 +85,7 @@
     x_peer = (chan + 2) % chans
     diag = (core_peer + 2) % chans
     others = (core_peer, x_peer, diag)
+    far_first = sorted(range(1, shards), key=lambda d: -min(d, shards - d))
 
     own_columns = pl.ds(pl.multiple_of(chan * LANES, LANES), LANES)
     loads = [(lfilt_a, lfilt), (tok, tbuf.at[chan]), (tok.at[pl.ds(count - RIM, RIM)], tmini.at[chan])]
@@ -105,6 +106,28 @@
         return carry
 
     lax.fori_loop(1, shards, greet, 0)
+
+    def spread(turned, block):
+        for dest in range(shards):
+            stage[dest, block * cd:(block + 1) * cd, :] = turned[dest * cd:(dest + 1) * cd, :]
+
+    def pack(dst, part, pieces):
+        size = blocks // pieces * cd
+        span = slice(part * size, (part + 1) * size)
+        dst[:, span, :] = stage[:, span, :].astype(BF16)
+
+    copies[0].wait()
+    for block in range(blocks):
+        spread(lfilt[block * LANES:(block + 1) * LANES, :].T, block)
+    pack(hs, 0, 1)
+    for copy in copies[1:]:
+        copy.wait()
+    gain_rows[...] = jnp.broadcast_to(gain[...], (LANES, LANES)).T
+    outer_t[...] = outer_f[...].astype(BF16)
+    for table, ref in ((ahead_f, ahead_t), (back_f, back_t), (close_f, close_t)):
+        high, low = split(table[...])
+        ref[0] = high
+        ref[1] = low
     pl.semaphore_wait(barrier, len(others) + shards - 1)
 
     def remote(src, dst, send, recv, device):
@@ -133,20 +156,20 @@
         columns = pl.ds(pl.multiple_of(peer * LANES, LANES), LANES)
         return remote(w_out.at[:, columns], wbuf.at[owner], wo_send.at[slot], wo_recv.at[owner], (seq, peer))
 
-    def swap(src, dst, send, recv, part, span, peer, owner):
-        return remote(src.at[peer, span], dst.at[owner, span], send.at[part, peer], recv.at[part, owner], (peer, chan))
-
     def swap_all(action, src, dst, send, recv, part, span):
-        def one(d, carry):
-            peer = (seq + d) % shards
-            if action == "start":
-                swap(src, dst, send, recv, part, span, peer, seq).start()
-            elif action == "recv":
-                swap(src, dst, send, recv, part, span, peer, peer).wait_recv()
-            else:
-                swap(src, dst, send, recv, part, span, peer, seq).wait_send()
-            return carry
-        lax.fori_loop(1, shards, one, 0)
+        if action == "start":
+            for d in far_first:
+                peer = (seq + d) % shards
+                remote(src.at[peer, span], dst.at[seq, span], send.at[part], recv.at[part], (peer, chan)).start()
+            return
+        several = pl.ds(0, shards - 1)
+        whole = remote(
+            src.at[several, span], dst.at[several, span], send.at[part], recv.at[part], ((seq + 1) % shards, chan)
+        )
+        if action == "recv":
+            whole.wait_recv()
+        else:
+            whole.wait_send()
 
     def h_swap(action, half):
         size = blocks // 2 * cd
@@ -159,27 +182,11 @@
     def y_swap(action, g):
         swap_all(action, ys.at[g], yr.at[g], y_send, y_recv, g, pl.ds(0, group * blocks))
 
-    def spread(turned, block):
-        for dest in range(shards):
-            stage[dest, block * cd:(block + 1) * cd, :] = turned[dest * cd:(dest + 1) * cd, :]
-
-    def pack(dst, part, pieces):
-        size = blocks // pieces * cd
-        span = slice(part * size, (part + 1) * size)
-        dst[:, span, :] = stage[:, span, :].astype(BF16)
-
-    copies[0].wait()
     for half in range(2):
-        for block in range(half * blocks // 2, (half + 1) * blocks // 2):
-            spread(lfilt[block * LANES:(block + 1) * LANES, :].T, block)
-        pack(hs, half, 2)
         h_swap("start", half)
     hr[seq] = hs[seq]
     for slot, peer in enumerate(others):
         wo_copy(slot, peer, chan).start()
-    for copy in copies[1:]:
-        copy.wait()
-    gain_rows = jnp.broadcast_to(gain[...], (LANES, LANES)).T
 
     def shorten(k):
         for g in range(3):
@@ -200,7 +207,7 @@
             block = k * (rows // LANES) + j
             turned = held[j * LANES:(j + 1) * LANES, :].T
             spread(turned, block)
-            skip_t[block * LANES:(block + 1) * LANES, :] = turned * gain_rows
+            skip_t[block * LANES:(block + 1) * LANES, :] = turned * gain_rows[...]
 
     def rim_copy():
         return remote(rim_out, rim_in, rim_send, rim_recv, ((seq + 1) % shards, chan))
@@ -215,11 +222,6 @@
     tail = jnp.concatenate([tmini[j] for j in range(chans)], axis=1)
     rim_out[...] = dot(tail, w[...]).astype(BF16)
     rim_copy().start()
-    outer_t[...] = outer_f[...].astype(BF16)
-    for table, ref in ((ahead_f, ahead_t), (back_f, back_t), (close_f, close_t)):
-        high, low = split(table[...])
-        ref[0] = high
-        ref[1] = low
     for k in range(chunks):
         take(k + 1)
         features = jnp.concatenate([tbuf[j, k * rows:(k + 1) * rows, :] for j in range(chans)], axis=1)
@@ -240,7 +242,7 @@
     padded = turn_t.shape[1]
     edge = group * padded
 
-    def spectrum(ref, g):
+    def spectrum(ref, g, product):
         columns = [ref[pl.ds(g * group + j, height, stride=cd), :].astype(BF16) for j in range(group)]
         signal = jnp.concatenate(columns, axis=1)
         signal = jnp.concatenate([signal, signal], axis=0)
@@ -251,13 +253,16 @@
             real = opened[:padded, j * LANES:(j + 1) * LANES]
             imag = opened[padded:, j * LANES:(j + 1) * LANES]
             turned.append(jnp.concatenate([real * cosine - imag * sine, real * sine + imag * cosine], axis=1))
-        return dot3(jnp.concatenate(turned, axis=0), ahead_t)
+        return product(jnp.concatenate(turned, axis=0), ahead_t)
+
+    def dot1(left, table_ref):
+        return dot(left.astype(BF16), table_ref[0])
 
     for half in range(2):
         h_swap("recv", half)
     h32[...] = hr[...].reshape(h32.shape).astype(F32)
     for g in range(groups):
-        hspec[g] = spectrum(h32, g)
+        hspec[g] = spectrum(h32, g, dot2)
     for block in range(blocks):
         span = slice(block * LANES, (block + 1) * LANES)
         keep_t[span, :] = keep[span, :].T
@@ -267,26 +272,37 @@
         w32[...] = wbuf[j].astype(F32)
         for g in range(groups):
             picked = [w32[pl.ds(g * group + c, shards, stride=cd), :] for c in range(group)]
-            wt[g, j] = jnp.concatenate(picked, axis=0).astype(BF16)
+            w_rows[g, j] = jnp.concatenate(picked, axis=0)
+    for g in range(groups):
+        wt[g] = jnp.concatenate([w_rows[g, j] for j in range(chans)], axis=0).T.astype(BF16)
+
+    for k in range(chunks + 1):
+        tok_copy(k, 1, x_peer, chan).wait_send()
+        tok_copy(k, 0, core_peer, chan).wait_send()
+        fwd_copy(k, x_peer).wait_send()
+    for slot, peer in enumerate(others):
+        wo_copy(slot, peer, chan).wait_send()
+    rim_copy().wait_send()
+    for half in range(2):
+        h_swap("send", half)
 
     for part in range(parts):
         x_swap("recv", part)
     x32[...] = xr[...].reshape(x32.shape).astype(F32)
 
     def convolve(g):
-        spectra = spectrum(x32, g)
+        spectra = spectrum(x32, g, dot1)
         xr_, xi_ = spectra[:, :LANES], spectra[:, LANES:]
         hr_, hi_ = hspec[g, :, :LANES], hspec[g, :, LANES:]
         product = jnp.concatenate([xr_ * hr_ - xi_ * hi_, xr_ * hi_ + xi_ * hr_], axis=1)
-        back = dot3(product, back_t)
+        back = dot1(product, back_t)
         cosine, sine = turn_t[0], turn_t[1]
         sums = []
         for j in range(group):
             real = back[j * padded:(j + 1) * padded, :LANES]
             imag = back[j * padded:(j + 1) * padded, LANES:]
             sums.append(jnp.concatenate([real * cosine + imag * sine, imag * cosine - real * sine], axis=0))
-        high, low = split(jnp.concatenate(sums, axis=1))
-        conv = dot(close_t[0], high) + (dot(close_t[0], low) + dot(close_t[1], high))
+        conv = dot(close_t[0], jnp.concatenate(sums, axis=1).astype(BF16))
         for j in range(group):
             y32[:, j * blocks:(j + 1) * blocks, :] = conv[:, j * LANES:(j + 1) * LANES].reshape(shards, blocks, LANES)
         ys[g] = y32[...].astype(BF16)
@@ -320,8 +336,7 @@
         gated_copy(g, 0, core_peer, core_peer).wait_recv()
         gated_copy(g, 0, core_peer, diag).wait_recv()
         whole = jnp.concatenate([gbuf[j, g] for j in range(chans)], axis=0)
-        weights = jnp.concatenate([wt[g, j] for j in range(chans)], axis=0)
-        part = dot(weights.astype(F32).T.astype(BF16), whole)
+        part = dot(wt[g], whole)
         if g > 0:
             part = part + acc[...]
         if g < groups - 1:
@@ -337,7 +352,11 @@
             gate(g - 1)
         if g >= 2:
             forward(g - 2)
+    for part in range(parts):
+        x_swap("send", part)
     gate(groups - 1)
+    for g in range(groups):
+        y_swap("send", g)
     for g in range(max(groups - 2, 0), groups - 1):
         forward(g)
     for g in range(groups - 2):
@@ -346,19 +365,7 @@
     for g in range(max(groups - 2, 0), groups):
         mix(g)
 
-    for k in range(chunks + 1):
-        tok_copy(k, 1, x_peer, chan).wait_send()
-        tok_copy(k, 0, core_peer, chan).wait_send()
-        fwd_copy(k, x_peer).wait_send()
-    for slot, peer in enumerate(others):
-        wo_copy(slot, peer, chan).wait_send()
-    rim_copy().wait_send()
-    for half in range(2):
-        h_swap("send", half)
-    for part in range(parts):
-        x_swap("send", part)
     for g in range(groups):
-        y_swap("send", g)
         gated_copy(g, 1, x_peer, chan).wait_send()
         gated_copy(g, 0, core_peer, chan).wait_send()
         gated_fwd(g, x_peer).wait_send()
@@ -424,14 +431,16 @@
             vmem((chans, groups, group * shards, count), BF16),
             vmem((chans, width, LANES), BF16),
             vmem((width, LANES), F32),
-            vmem((groups, chans, group * shards, LANES), BF16),
+            vmem((groups, chans, group * shards, LANES), F32),
+            vmem((groups, LANES, chans * group * shards), BF16),
             vmem((LANES, count), F32),
+            vmem((LANES, LANES), F32),
             dma((14,)),
             dma((2, chunks + 1)), dma((chans, chunks + 1)), dma((chunks + 1,)),
             dma((3,)), dma((chans,)), dma, dma,
-            dma((2, shards)), dma((2, shards)),
-            dma((parts, shards)), dma((parts, shards)),
-            dma((groups, shards)), dma((groups, shards)),
+            dma((2,)), dma((2,)),
+            dma((parts,)), dma((parts,)),
+            dma((groups,)), dma((groups,)),
             dma((2, groups)), dma((chans, groups)), dma((groups,)),
         ],
         compiler_params=pltpu.CompilerParams(

time: 45.6 us -> 42.5 us (0.932)
  Pallas kernels: 43.8 us -> 40.7 us
    pallas_call x1, Pallas kernels: 43.8 us -> 40.7 us  [on_device(): pl.pallas_call(functools.partial(kernel, shards, chans, chunks, parts, gr...]
where the time goes in v3:
time: 42.5 us; the launch traced here: 42.4 us
  Pallas kernels  40.7 us (96%)
  local copies, waits for them, and re-layouts  1.67 us (4%)
    pallas_call x1, Pallas kernels, on_device(): pl.pallas_call(functools.partial(kernel, shards, chans, chunks, parts, gr...  40.7 us
    unnamed x1, local copies, waits for them, and re-layouts  1.67 us

profile of v3, /device:TPU:1, one launch (start us, length us, event | category | flops | bytes accessed | tf_op | source)
XLA Modules:
  0.0 42.4 jit_solution(1231407457739107966)
XLA Ops:
  0.0 40.7 %shard_map.109 = bf16[1024,128]{1,0:T(8,128)(2,1)} custom-call(bf16[1024,128]{1,0:T(8,128)(2,1)} %tok.1, bf16[3,512,128]{2,1,0:T(8,128)(2,1)} %bitcast.2, f32[3,3,128]{2,1,0:T(4,128)} %sfilt_a.1, f32[1024,128]{1,0:T(8,128)} %lfilt_a.1, f32[1,128]{1,0:T(1,128)} %bitcast.3, bf16[128,512]{1,0:T(8,128)(2,1)} %w_out.1, f32[160,128]{1,0:T(8,128)} %constant.10.clone.outer_a, ...), custom_call_target="tpu_custom_call" | custom-call | flops 4000000000 | bytes 4000000 | tf_op jit(solution)/shard_map/pallas_call | solution.py:396
  40.7 1.7 %copy.13 = bf16[1024,128]{1,0:T(8,128)(2,1)} copy(bf16[1024,128]{1,0:T(8,128)(2,1)} %shard_map.109) | data formatting | bytes 524288

commit v4 on v3

--- a/solution.py
+++ b/solution.py
@@ -58,6 +58,18 @@
     return jnp.dot(left, right, preferred_element_type=F32)
 
 
+def each(low, high, body):
+    def one(i, carry):
+        body(i)
+        return carry
+
+    lax.fori_loop(low, high, one, 0)
+
+
+def piece(start, size):
+    return pl.ds(pl.multiple_of(start, size), size)
+
+
 def dot2(left, table_ref):
     rounded = left.astype(BF16)
     return dot(rounded, table_ref[0]) + dot(rounded, table_ref[1])
@@ -100,25 +112,22 @@
     for peer in others:
         pl.semaphore_signal(barrier, inc=1, device_id=(seq, peer), device_id_type=MESH)
 
-    def greet(d, carry):
+    @functools.partial(each, 1, shards)
+    def greet(d):
         peer = (seq + d) % shards
         pl.semaphore_signal(barrier, inc=1, device_id=(peer, chan), device_id_type=MESH)
-        return carry
-
-    lax.fori_loop(1, shards, greet, 0)
 
     def spread(turned, block):
         for dest in range(shards):
-            stage[dest, block * cd:(block + 1) * cd, :] = turned[dest * cd:(dest + 1) * cd, :]
+            stage[dest, piece(block * cd, cd), :] = turned[dest * cd:(dest + 1) * cd, :]
 
     def pack(dst, part, pieces):
         size = blocks // pieces * cd
-        span = slice(part * size, (part + 1) * size)
+        span = piece(part * size, size)
         dst[:, span, :] = stage[:, span, :].astype(BF16)
 
     copies[0].wait()
-    for block in range(blocks):
-        spread(lfilt[block * LANES:(block + 1) * LANES, :].T, block)
+    each(0, blocks, lambda block: spread(lfilt[piece(block * LANES, LANES), :].T, block))
     pack(hs, 0, 1)
     for copy in copies[1:]:
         copy.wait()
@@ -136,21 +145,27 @@
             device_id=device, device_id_type=MESH,
         )
 
+    def first(k):
+        return isinstance(k, int) and k == 0
+
     def landing(k, owner):
-        if k == 0:
+        if first(k):
             return tmini.at[owner]
-        return tbuf.at[owner, pl.ds((k - 1) * rows, rows)]
+        return tbuf.at[owner, piece((k - 1) * rows, rows)]
 
     def tok_copy(k, slot, peer, owner):
-        span = pl.ds(count - RIM, RIM) if k == 0 else pl.ds((k - 1) * rows, rows)
+        span = pl.ds(count - RIM, RIM) if first(k) else piece((k - 1) * rows, rows)
         return remote(tok.at[span], landing(k, owner), tok_send.at[slot, k], tok_recv.at[owner, k], (seq, peer))
 
     def fwd_copy(k, owner):
         return remote(landing(k, owner), landing(k, owner), fwd_send.at[k], tok_recv.at[owner, k], (seq, core_peer))
 
-    for k in range(chunks + 1):
+    def give(k):
         tok_copy(k, 1, x_peer, chan).start()
         tok_copy(k, 0, core_peer, chan).start()
+
+    give(0)
+    each(1, chunks + 1, give)
 
     def wo_copy(slot, peer, owner):
         columns = pl.ds(pl.multiple_of(peer * LANES, LANES), LANES)
@@ -177,7 +192,7 @@
 
     def x_swap(action, part):
         size = blocks // parts * cd
-        swap_all(action, xs, xr, x_send, x_recv, part, pl.ds(part * size, size))
+        swap_all(action, xs, xr, x_send, x_recv, part, piece(part * size, size))
 
     def y_swap(action, g):
         swap_all(action, ys.at[g], yr.at[g], y_send, y_recv, g, pl.ds(0, group * blocks))
@@ -191,23 +206,24 @@
     def shorten(k):
         for g in range(3):
             lanes = slice(g * LANES, (g + 1) * LANES)
-            base = RIM + k * rows
+            base = pl.multiple_of(RIM // 2 + k * rows, 8)
+            window = proj[pl.ds(base, rows + 8), lanes]
             value = (
-                sfilt[0, g:g + 1, :] * proj[base:base + rows, lanes]
-                + sfilt[1, g:g + 1, :] * proj[base - 1:base - 1 + rows, lanes]
-                + sfilt[2, g:g + 1, :] * proj[base - 2:base - 2 + rows, lanes]
+                sfilt[0, g:g + 1, :] * window[8:, :]
+                + sfilt[1, g:g + 1, :] * window[7:-1, :]
+                + sfilt[2, g:g + 1, :] * window[6:-2, :]
             )
             if g == 0:
                 held = value
             elif g == 1:
                 held = held * value
             else:
-                keep[k * rows:(k + 1) * rows, :] = value
+                keep[piece(k * rows, rows), :] = value
         for j in range(rows // LANES):
             block = k * (rows // LANES) + j
             turned = held[j * LANES:(j + 1) * LANES, :].T
             spread(turned, block)
-            skip_t[block * LANES:(block + 1) * LANES, :] = turned * gain_rows[...]
+            skip_t[piece(block * LANES, LANES), :] = turned * gain_rows[...]
 
     def rim_copy():
         return remote(rim_out, rim_in, rim_send, rim_recv, ((seq + 1) % shards, chan))
@@ -222,20 +238,25 @@
     tail = jnp.concatenate([tmini[j] for j in range(chans)], axis=1)
     rim_out[...] = dot(tail, w[...]).astype(BF16)
     rim_copy().start()
-    for k in range(chunks):
-        take(k + 1)
-        features = jnp.concatenate([tbuf[j, k * rows:(k + 1) * rows, :] for j in range(chans)], axis=1)
-        projected = dot(features, w[...]).astype(BF16)
-        proj[RIM + k * rows:RIM + (k + 1) * rows, :] = projected.astype(F32)
-        if k == 0:
-            rim_copy().wait_recv()
-            live = (seq > 0).astype(F32)
-            proj[0:RIM, :] = rim_in[...].astype(F32) * live
-        shorten(k)
-        if (k + 1) * parts % chunks == 0:
-            part = (k + 1) * parts // chunks - 1
-            pack(xs, part, parts)
-            x_swap("start", part)
+    @functools.partial(each, 0, parts)
+    def project(part):
+        for i in range(chunks // parts):
+            k = part * (chunks // parts) + i
+            take(k + 1)
+            span = piece(k * rows, rows)
+            features = jnp.concatenate([tbuf[j, span, :] for j in range(chans)], axis=1)
+            projected = dot(features, w[...]).astype(BF16)
+            proj[pl.ds(pl.multiple_of(RIM + k * rows, RIM), rows), :] = projected.astype(F32)
+            if i == 0:
+                @pl.when(part == 0)
+                def edge_rows():
+                    rim_copy().wait_recv()
+                    live = (seq > 0).astype(F32)
+                    proj[0:RIM, :] = rim_in[...].astype(F32) * live
+            shorten(k)
+        pack(xs, part, parts)
+        x_swap("start", part)
+
     xr[seq] = xs[seq]
 
     height = shards * blocks
@@ -261,25 +282,38 @@
     for half in range(2):
         h_swap("recv", half)
     h32[...] = hr[...].reshape(h32.shape).astype(F32)
-    for g in range(groups):
+
+    @functools.partial(each, 0, groups)
+    def filter_spectra(g):
         hspec[g] = spectrum(h32, g, dot2)
-    for block in range(blocks):
-        span = slice(block * LANES, (block + 1) * LANES)
+
+    @functools.partial(each, 0, blocks)
+    def turn_gate(block):
+        span = piece(block * LANES, LANES)
         keep_t[span, :] = keep[span, :].T
+
     for slot, peer in enumerate(others):
         wo_copy(slot, peer, peer).wait_recv()
-    for j in range(chans):
+
+    @functools.partial(each, 0, chans)
+    def turn_weights(j):
         w32[...] = wbuf[j].astype(F32)
         for g in range(groups):
             picked = [w32[pl.ds(g * group + c, shards, stride=cd), :] for c in range(group)]
             w_rows[g, j] = jnp.concatenate(picked, axis=0)
-    for g in range(groups):
+
+    @functools.partial(each, 0, groups)
+    def pack_weights(g):
         wt[g] = jnp.concatenate([w_rows[g, j] for j in range(chans)], axis=0).T.astype(BF16)
 
-    for k in range(chunks + 1):
+    def settle(k):
         tok_copy(k, 1, x_peer, chan).wait_send()
         tok_copy(k, 0, core_peer, chan).wait_send()
         fwd_copy(k, x_peer).wait_send()
+
+    settle(0)
+    each(1, chunks + 1, settle)
+    acc[...] = jnp.zeros_like(acc)
     for slot, peer in enumerate(others):
         wo_copy(slot, peer, chan).wait_send()
     rim_copy().wait_send()
@@ -336,36 +370,25 @@
         gated_copy(g, 0, core_peer, core_peer).wait_recv()
         gated_copy(g, 0, core_peer, diag).wait_recv()
         whole = jnp.concatenate([gbuf[j, g] for j in range(chans)], axis=0)
-        part = dot(wt[g], whole)
-        if g > 0:
-            part = part + acc[...]
-        if g < groups - 1:
-            acc[...] = part
-        else:
-            for block in range(blocks):
-                span = slice(block * LANES, (block + 1) * LANES)
-                out[span, :] = part[:, span].T.astype(BF16)
-
-    for g in range(groups):
-        convolve(g)
-        if g >= 1:
-            gate(g - 1)
-        if g >= 2:
-            forward(g - 2)
-    for part in range(parts):
-        x_swap("send", part)
-    gate(groups - 1)
-    for g in range(groups):
-        y_swap("send", g)
-    for g in range(max(groups - 2, 0), groups - 1):
-        forward(g)
-    for g in range(groups - 2):
-        mix(g)
+        acc[...] += dot(wt[g], whole)
+
+    @functools.partial(each, 0, groups + 1)
+    def stream(g):
+        pl.when(g < groups)(lambda: convolve(g))
+        pl.when(g >= 1)(lambda: gate(g - 1))
+        pl.when(g >= 2)(lambda: forward(g - 2))
+        pl.when(g >= 3)(lambda: mix(g - 3))
+
     forward(groups - 1)
-    for g in range(max(groups - 2, 0), groups):
-        mix(g)
-
-    for g in range(groups):
+    each(0, parts, lambda part: x_swap("send", part))
+    each(0, groups, lambda g: y_swap("send", g))
+    each(max(groups - 2, 0), groups, mix)
+    for block in range(blocks):
+        span = slice(block * LANES, (block + 1) * LANES)
+        out[span, :] = acc[:, span].T.astype(BF16)
+
+    @functools.partial(each, 0, groups)
+    def finish(g):
         gated_copy(g, 1, x_peer, chan).wait_send()
         gated_copy(g, 0, core_peer, chan).wait_send()
         gated_fwd(g, x_peer).wait_send()

time: 42.5 us -> 43.1 us (1.014)
  Pallas kernels: 40.7 us -> 41.3 us
    pallas_call x1, Pallas kernels: 40.7 us -> 41.3 us  [on_device(): pl.pallas_call(functools.partial(kernel, shards, chans, chunks, parts, gr...]
where the time goes in v4:
time: 43.1 us; the launch traced here: 43 us
  Pallas kernels  41.3 us (96%)
  local copies, waits for them, and re-layouts  1.67 us (4%)
    pallas_call x1, Pallas kernels, on_device(): pl.pallas_call(functools.partial(kernel, shards, chans, chunks, parts, gr...  41.3 us
    unnamed x1, local copies, waits for them, and re-layouts  1.67 us

profile of v4, /device:TPU:1, one launch (start us, length us, event | category | flops | bytes accessed | tf_op | source)
XLA Modules:
  0.0 43.0 jit_solution(13602314662063609530)
XLA Ops:
  0.0 41.3 %shard_map.109 = bf16[1024,128]{1,0:T(8,128)(2,1)} custom-call(bf16[1024,128]{1,0:T(8,128)(2,1)} %tok.1, bf16[3,512,128]{2,1,0:T(8,128)(2,1)} %bitcast.2, f32[3,3,128]{2,1,0:T(4,128)} %sfilt_a.1, f32[1024,128]{1,0:T(8,128)} %lfilt_a.1, f32[1,128]{1,0:T(1,128)} %bitcast.3, bf16[128,512]{1,0:T(8,128)(2,1)} %w_out.1, f32[160,128]{1,0:T(8,128)} %constant.10.clone.outer_a, ...), custom_call_target="tpu_custom_call" | custom-call | flops 4000000000 | bytes 4000000 | tf_op jit(solution)/shard_map/pallas_call | solution.py:419
  41.3 1.7 %copy.13 = bf16[1024,128]{1,0:T(8,128)(2,1)} copy(bf16[1024,128]{1,0:T(8,128)(2,1)} %shard_map.109) | data formatting | bytes 524288

commit v5 on v4

--- a/solution.py
+++ b/solution.py
@@ -186,9 +186,8 @@
         else:
             whole.wait_send()
 
-    def h_swap(action, half):
-        size = blocks // 2 * cd
-        swap_all(action, hs, hr, h_send, h_recv, half, pl.ds(half * size, size))
+    def h_swap(action):
+        swap_all(action, hs, hr, h_send, h_recv, 0, pl.ds(0, blocks * cd))
 
     def x_swap(action, part):
         size = blocks // parts * cd
@@ -197,8 +196,7 @@
     def y_swap(action, g):
         swap_all(action, ys.at[g], yr.at[g], y_send, y_recv, g, pl.ds(0, group * blocks))
 
-    for half in range(2):
-        h_swap("start", half)
+    h_swap("start")
     hr[seq] = hs[seq]
     for slot, peer in enumerate(others):
         wo_copy(slot, peer, chan).start()
@@ -279,8 +277,7 @@
     def dot1(left, table_ref):
         return dot(left.astype(BF16), table_ref[0])
 
-    for half in range(2):
-        h_swap("recv", half)
+    h_swap("recv")
     h32[...] = hr[...].reshape(h32.shape).astype(F32)
 
     @functools.partial(each, 0, groups)
@@ -317,8 +314,7 @@
     for slot, peer in enumerate(others):
         wo_copy(slot, peer, chan).wait_send()
     rim_copy().wait_send()
-    for half in range(2):
-        h_swap("send", half)
+    h_swap("send")
 
     for part in range(parts):
         x_swap("recv", part)
@@ -400,8 +396,8 @@
     blocks = count // LANES
     cd = width // shards
     chunks = 4
-    parts = 4 if blocks // 4 * cd % 16 == 0 else 2
-    group = min(cd, 4)
+    parts = 2
+    group = min(cd, 8)
     groups = cd // group
     consts = tables(2 * length)
     outer, turn, ahead, back, close = consts
@@ -461,7 +457,7 @@
             dma((14,)),
             dma((2, chunks + 1)), dma((chans, chunks + 1)), dma((chunks + 1,)),
             dma((3,)), dma((chans,)), dma, dma,
-            dma((2,)), dma((2,)),
+            dma((1,)), dma((1,)),
             dma((parts,)), dma((parts,)),
             dma((groups,)), dma((groups,)),
             dma((2, groups)), dma((chans, groups)), dma((groups,)),

time: 43.1 us -> 42.2 us (0.979)
  Pallas kernels: 41.3 us -> 40.4 us
    pallas_call x1, Pallas kernels: 41.3 us -> 40.4 us  [on_device(): pl.pallas_call(functools.partial(kernel, shards, chans, chunks, parts, gr...]
where the time goes in v5:
time: 42.2 us; the launch traced here: 42.1 us
  Pallas kernels  40.4 us (96%)
  local copies, waits for them, and re-layouts  1.67 us (4%)
    pallas_call x1, Pallas kernels, on_device(): pl.pallas_call(functools.partial(kernel, shards, chans, chunks, parts, gr...  40.4 us
    unnamed x1, local copies, waits for them, and re-layouts  1.67 us

profile of v5, /device:TPU:1, one launch (start us, length us, event | category | flops | bytes accessed | tf_op | source)
XLA Modules:
  0.0 42.1 jit_solution(8512979421204712015)
XLA Ops:
  0.0 40.4 %shard_map.109 = bf16[1024,128]{1,0:T(8,128)(2,1)} custom-call(bf16[1024,128]{1,0:T(8,128)(2,1)} %tok.1, bf16[3,512,128]{2,1,0:T(8,128)(2,1)} %bitcast.2, f32[3,3,128]{2,1,0:T(4,128)} %sfilt_a.1, f32[1024,128]{1,0:T(8,128)} %lfilt_a.1, f32[1,128]{1,0:T(1,128)} %bitcast.3, bf16[128,512]{1,0:T(8,128)(2,1)} %w_out.1, f32[160,128]{1,0:T(8,128)} %constant.10.clone.outer_a, ...), custom_call_target="tpu_custom_call" | custom-call | flops 4000000000 | bytes 4000000 | tf_op jit(solution)/shard_map/pallas_call | solution.py:415
  40.4 1.7 %copy.13 = bf16[1024,128]{1,0:T(8,128)(2,1)} copy(bf16[1024,128]{1,0:T(8,128)(2,1)} %shard_map.109) | data formatting | bytes 524288

commit v6 on v5

--- a/solution.py
+++ b/solution.py
@@ -81,7 +81,7 @@
     out,
     tbuf, tmini, w, sfilt, lfilt, gain, outer_f, turn_t, ahead_f, back_f, close_f,
     outer_t, ahead_t, back_t, close_t,
-    proj, rim_out, rim_in, keep, keep_t, skip_t, stage, hs, hr, xs, xr, ys, yr,
+    proj, rim_out, rim_in, keep, keep_t, skip_t, stage, h_stage, hs, hr, xs, xr, ys, yr,
     x32, h32, hspec, y32, c32, gbuf, wbuf, w32, w_rows, wt, acc, gain_rows,
     local, tok_send, tok_recv, fwd_send, wo_send, wo_recv, rim_send, rim_recv,
     h_send, h_recv, x_send, x_recv, y_send, y_recv, g_send, g_recv, gf_send,
@@ -127,8 +127,15 @@
         dst[:, span, :] = stage[:, span, :].astype(BF16)
 
     copies[0].wait()
-    each(0, blocks, lambda block: spread(lfilt[piece(block * LANES, LANES), :].T, block))
-    pack(hs, 0, 1)
+    @functools.partial(each, 0, blocks)
+    def spread_filter(block):
+        turned = lfilt[piece(block * LANES, LANES), :].T
+        for dest in range(shards):
+            for g in range(groups):
+                start = dest * cd + g * group
+                h_stage[g, dest, piece(block * group, group), :] = turned[start:start + group, :]
+
+    hs[...] = h_stage[...].astype(BF16)
     for copy in copies[1:]:
         copy.wait()
     gain_rows[...] = jnp.broadcast_to(gain[...], (LANES, LANES)).T
@@ -186,8 +193,8 @@
         else:
             whole.wait_send()
 
-    def h_swap(action):
-        swap_all(action, hs, hr, h_send, h_recv, 0, pl.ds(0, blocks * cd))
+    def h_swap(action, g):
+        swap_all(action, hs.at[g], hr.at[g], h_send, h_recv, g, pl.ds(0, blocks * group))
 
     def x_swap(action, part):
         size = blocks // parts * cd
@@ -196,8 +203,9 @@
     def y_swap(action, g):
         swap_all(action, ys.at[g], yr.at[g], y_send, y_recv, g, pl.ds(0, group * blocks))
 
-    h_swap("start")
-    hr[seq] = hs[seq]
+    h_swap("start", 0)
+    for g in range(groups):
+        hr[g, seq] = hs[g, seq]
     for slot, peer in enumerate(others):
         wo_copy(slot, peer, chan).start()
 
@@ -254,15 +262,20 @@
             shorten(k)
         pack(xs, part, parts)
         x_swap("start", part)
-
+        for j in range(blocks // parts):
+            span = piece((part * (blocks // parts) + j) * LANES, LANES)
+            keep_t[span, :] = keep[span, :].T
+
+    for g in range(1, groups):
+        h_swap("start", g)
     xr[seq] = xs[seq]
 
     height = shards * blocks
     padded = turn_t.shape[1]
     edge = group * padded
 
-    def spectrum(ref, g, product):
-        columns = [ref[pl.ds(g * group + j, height, stride=cd), :].astype(BF16) for j in range(group)]
+    def spectrum(ref, start, stride, product):
+        columns = [ref[pl.ds(start + j, height, stride=stride), :].astype(BF16) for j in range(group)]
         signal = jnp.concatenate(columns, axis=1)
         signal = jnp.concatenate([signal, signal], axis=0)
         opened = dot(outer_t[...], signal)
@@ -277,51 +290,20 @@
     def dot1(left, table_ref):
         return dot(left.astype(BF16), table_ref[0])
 
-    h_swap("recv")
-    h32[...] = hr[...].reshape(h32.shape).astype(F32)
-
-    @functools.partial(each, 0, groups)
     def filter_spectra(g):
-        hspec[g] = spectrum(h32, g, dot2)
-
-    @functools.partial(each, 0, blocks)
-    def turn_gate(block):
-        span = piece(block * LANES, LANES)
-        keep_t[span, :] = keep[span, :].T
-
-    for slot, peer in enumerate(others):
-        wo_copy(slot, peer, peer).wait_recv()
-
-    @functools.partial(each, 0, chans)
-    def turn_weights(j):
-        w32[...] = wbuf[j].astype(F32)
-        for g in range(groups):
-            picked = [w32[pl.ds(g * group + c, shards, stride=cd), :] for c in range(group)]
-            w_rows[g, j] = jnp.concatenate(picked, axis=0)
-
-    @functools.partial(each, 0, groups)
-    def pack_weights(g):
-        wt[g] = jnp.concatenate([w_rows[g, j] for j in range(chans)], axis=0).T.astype(BF16)
-
-    def settle(k):
-        tok_copy(k, 1, x_peer, chan).wait_send()
-        tok_copy(k, 0, core_peer, chan).wait_send()
-        fwd_copy(k, x_peer).wait_send()
-
-    settle(0)
-    each(1, chunks + 1, settle)
+        h_swap("recv", g)
+        h32[...] = hr[g].reshape(h32.shape).astype(F32)
+        hspec[g] = spectrum(h32, 0, group, dot2)
+
+    filter_spectra(0)
     acc[...] = jnp.zeros_like(acc)
-    for slot, peer in enumerate(others):
-        wo_copy(slot, peer, chan).wait_send()
-    rim_copy().wait_send()
-    h_swap("send")
 
     for part in range(parts):
         x_swap("recv", part)
     x32[...] = xr[...].reshape(x32.shape).astype(F32)
 
     def convolve(g):
-        spectra = spectrum(x32, g, dot1)
+        spectra = spectrum(x32, g * group, cd, dot1)
         xr_, xi_ = spectra[:, :LANES], spectra[:, LANES:]
         hr_, hi_ = hspec[g, :, :LANES], hspec[g, :, LANES:]
         product = jnp.concatenate([xr_ * hr_ - xi_ * hi_, xr_ * hi_ + xi_ * hr_], axis=1)
@@ -368,11 +350,40 @@
         whole = jnp.concatenate([gbuf[j, g] for j in range(chans)], axis=0)
         acc[...] += dot(wt[g], whole)
 
+    def meanwhile():
+        for slot, peer in enumerate(others):
+            wo_copy(slot, peer, peer).wait_recv()
+
+        @functools.partial(each, 0, chans)
+        def turn_weights(j):
+            w32[...] = wbuf[j].astype(F32)
+            for g in range(groups):
+                picked = [w32[pl.ds(g * group + c, shards, stride=cd), :] for c in range(group)]
+                w_rows[g, j] = jnp.concatenate(picked, axis=0)
+
+        @functools.partial(each, 0, groups)
+        def pack_weights(g):
+            wt[g] = jnp.concatenate([w_rows[g, j] for j in range(chans)], axis=0).T.astype(BF16)
+
+        def settle(k):
+            tok_copy(k, 1, x_peer, chan).wait_send()
+            tok_copy(k, 0, core_peer, chan).wait_send()
+            fwd_copy(k, x_peer).wait_send()
+
+        settle(0)
+        each(1, chunks + 1, settle)
+        for slot, peer in enumerate(others):
+            wo_copy(slot, peer, chan).wait_send()
+        rim_copy().wait_send()
+        each(0, groups, lambda g: h_swap("send", g))
+
     @functools.partial(each, 0, groups + 1)
     def stream(g):
+        pl.when((g >= 1) & (g < groups))(lambda: filter_spectra(g))
         pl.when(g < groups)(lambda: convolve(g))
         pl.when(g >= 1)(lambda: gate(g - 1))
         pl.when(g >= 2)(lambda: forward(g - 2))
+        pl.when(g == groups - 1)(meanwhile)
         pl.when(g >= 3)(lambda: mix(g - 3))
 
     forward(groups - 1)
@@ -381,7 +392,7 @@
     each(max(groups - 2, 0), groups, mix)
     for block in range(blocks):
         span = slice(block * LANES, (block + 1) * LANES)
-        out[span, :] = acc[:, span].T.astype(BF16)
+        out[span, :] = acc[:, span].T
 
     @functools.partial(each, 0, groups)
     def finish(g):
@@ -414,7 +425,7 @@
     ) + tuple(jnp.asarray(c) for c in consts)
     return pl.pallas_call(
         functools.partial(kernel, shards, chans, chunks, parts, group),
-        out_shape=jax.ShapeDtypeStruct((count, width), BF16),
+        out_shape=jax.ShapeDtypeStruct((count, width), F32),
         in_specs=[pl.BlockSpec(memory_space=pl.ANY)] * len(operands),
         out_specs=pl.BlockSpec(memory_space=vmem),
         scratch_shapes=[
@@ -436,14 +447,15 @@
             vmem((blocks * LANES, LANES), F32),
             vmem((blocks * LANES, LANES), F32),
             vmem(swap_shape, F32),
-            vmem(swap_shape, BF16),
-            vmem(swap_shape, BF16),
+            vmem(back_shape, F32),
+            vmem(back_shape, BF16),
+            vmem(back_shape, BF16),
             vmem(swap_shape, BF16),
             vmem(swap_shape, BF16),
             vmem(back_shape, BF16),
             vmem(back_shape, BF16),
             vmem(flat_shape, F32),
-            vmem(flat_shape, F32),
+            vmem((shards * group * blocks, LANES), F32),
             vmem((groups, group * turn.shape[1], 2 * LANES), F32),
             vmem(back_shape[1:], F32),
             vmem((shards * group * blocks, LANES), F32),
@@ -457,7 +469,7 @@
             dma((14,)),
             dma((2, chunks + 1)), dma((chans, chunks + 1)), dma((chunks + 1,)),
             dma((3,)), dma((chans,)), dma, dma,
-            dma((1,)), dma((1,)),
+            dma((groups,)), dma((groups,)),
             dma((parts,)), dma((parts,)),
             dma((groups,)), dma((groups,)),
             dma((2, groups)), dma((chans, groups)), dma((groups,)),
@@ -466,7 +478,7 @@
             collective_id=0, has_side_effects=True, vmem_limit_bytes=56 * 1024 * 1024
         ),
         cost_estimate=pl.CostEstimate(flops=4 * 10**9, bytes_accessed=4 * 10**6, transcendentals=0),
-    )(*operands)
+    )(*operands).astype(BF16)
 
 
 def solution(mesh):

time: 42.2 us -> 41.2 us (0.976)
  other arithmetic: 0 us -> 1.77 us
  local copies, waits for them, and re-layouts: 1.67 us -> 0 us
  Pallas kernels: 40.4 us -> 39.2 us
    convert_element_type x0 -> x1, other arithmetic: none -> 1.77 us  [on_device(): return pl.pallas_call(functools.partial(kernel, shards, chans, chunks, pa...]
    unnamed x1 -> x0, local copies, waits for them, and re-layouts: 1.67 us -> none
    pallas_call x1, Pallas kernels: 40.4 us -> 39.2 us  [on_device(): pl.pallas_call(functools.partial(kernel, shards, chans, chunks, parts, gr...]
where the time goes in v6:
time: 41.2 us; the launch traced here: 41 us
  Pallas kernels  39.2 us (95%)
  other arithmetic  1.77 us (4%)
    pallas_call x1, Pallas kernels, on_device(): pl.pallas_call(functools.partial(kernel, shards, chans, chunks, parts, gr...  39.2 us
    convert_element_type x1, other arithmetic, on_device(): return pl.pallas_call(functools.partial(kernel, shards, chans, chunks, pa...  1.77 us

profile of v6, /device:TPU:1, one launch (start us, length us, event | category | flops | bytes accessed | tf_op | source)
XLA Modules:
  0.0 41.0 jit_solution(15474514205917281906)
XLA Ops:
  0.0 39.2 %shard_map.109 = f32[1024,128]{1,0:T(8,128)} custom-call(bf16[1024,128]{1,0:T(8,128)(2,1)} %tok.1, bf16[3,512,128]{2,1,0:T(8,128)(2,1)} %bitcast.2, f32[3,3,128]{2,1,0:T(4,128)} %sfilt_a.1, f32[1024,128]{1,0:T(8,128)} %lfilt_a.1, f32[1,128]{1,0:T(1,128)} %bitcast.3, bf16[128,512]{1,0:T(8,128)(2,1)} %w_out.1, f32[160,128]{1,0:T(8,128)} %constant.10.clone.outer_a, ...), custom_call_target="tpu_custom_call" | custom-call | flops 4000000000 | bytes 4000000 | tf_op jit(solution)/shard_map/pallas_call | solution.py:426
  39.2 1.8 %convert_element_type.3 = bf16[1024,128]{1,0:T(8,128)(2,1)} convert(f32[1024,128]{1,0:T(8,128)} %shard_map.109) | non-fusion elementwise | flops 131072 | bytes 786432 | tf_op jit(solution)/shard_map/convert_element_type | solution.py:481
